TPU v7x, 32 devices: a whole 2x2x4 slice. The times are simulated.
32 devices in a mesh: leaf: 8 (over z, y), samp: 4 (over x, core).
Axes of the slice: x: 2, y: 2, z: 4, core: 2. Of those that a mesh axis runs over, the one named last changes fastest.
Arguments:
- samples: bfloat16 [32768, 256], P('leaf', 'samp'), may hold values from -6 to 6
- omega: bfloat16 [32768, 256], P('leaf', 'samp'), may hold values from -6 to 6
- leaf_basis: bfloat16 [256, 64, 128], P('leaf'), may hold values from -0.5 to 0.5
- near_blocks: bfloat16 [256, 8, 128, 128], P('leaf'), may hold values from -0.1875 to 0.1875
- near_index: int32 [256, 8], P('leaf'), may hold values from 0 to 255, as said below
- near_count: int32 [256], P('leaf'), may hold values from 2 to 8, as said below
- inner_transfer: bfloat16 [496, 4096], P('leaf'), may hold values from -0.5 to 0.5
- upper_transfer: bfloat16 [14, 4096], replicated, may hold values from -0.5 to 0.5
Outputs:
- leaf_coeffs: float32 [256, 64, 256], P('leaf', None, 'samp')
- leaf_gram: float32 [256, 4096], P('leaf', 'samp')
- ancestor_coeffs: float32 [8, 3, 64, 256], P('leaf', None, None, 'samp')
Inputs may be any that keep to these rules, and one draw needn't show every extreme that they name: `near_index`: slot 0 of leaf i names i itself, slot 1 names a leaf exactly 32 away from i, and every slot names a leaf at most 32 away from i. `near_count`: every group of 32 consecutive leaves has a leaf with all 8 slots live.
All inputs are finite; a program needn't handle non-finite values.
Results may differ from a plain program's by a relative error of at most 0.0029.
Values may be sent and summed in bfloat16 or wider, within the bound.
A program may use at most 64 MiB of HBM per device.

v0:
```python
import jax
import jax.numpy as jnp
from jax import lax
from jax.sharding import PartitionSpec as P


def with_halo(cells, sides, width):
    for axis, dim in sides:
        count = lax.axis_size(axis)
        ends = count - 1
        head = lax.slice_in_dim(cells, 0, width, axis=dim)
        tail = lax.slice_in_dim(cells, cells.shape[dim] - width, cells.shape[dim], axis=dim)
        cells = jnp.concatenate(
            [
                lax.ppermute(tail, axis, [(i, (i + 1) % count) for i in range(ends)]),
                cells,
                lax.ppermute(head, axis, [((i + 1) % count, i) for i in range(ends)]),
            ],
            axis=dim,
        )
    return cells


def partner(shard, axis, stride):
    return lax.ppermute(shard, axis, [(i, i ^ 1 << stride) for i in range(lax.axis_size(axis))])


def shards(
    samples, omega, leaf_basis, near_blocks, near_index, near_count, inner_transfer, upper_transfer
):
    leaf_count = near_count.shape[0]
    slot_count = near_index.shape[1]
    rank_size = leaf_basis.shape[1]
    leaf_size = leaf_basis.shape[2]
    column_count = samples.shape[1]
    widened = with_halo(omega, (("leaf", 0),), leaf_count * leaf_size)
    widened = widened.reshape(3 * leaf_count, leaf_size, column_count)
    device = lax.axis_index("leaf")
    anchor = device * leaf_count - leaf_count
    local_index = near_index - anchor
    fetched = widened[local_index]
    live_mask = (jnp.arange(slot_count)[None, :] < near_count[:, None]).astype(jnp.bfloat16)
    fetched = fetched * live_mask[:, :, None, None]
    near_sum = jnp.einsum(
        "gkab,gkbs->gas", near_blocks, fetched, preferred_element_type=jnp.float32
    )
    sample_rows = samples.reshape(leaf_count, leaf_size, column_count).astype(jnp.float32)
    far_part = (sample_rows - near_sum).astype(jnp.bfloat16)
    cluster_coefficient_array = jnp.einsum(
        "grb,gbs->grs", leaf_basis, far_part, preferred_element_type=jnp.float32
    )
    overall_column_count = column_count * lax.axis_size("samp")
    gram_term = (
        jnp.einsum(
            "ydb,ykb->ydk",
            cluster_coefficient_array,
            cluster_coefficient_array,
            precision=lax.Precision.HIGHEST,
        )
        / overall_column_count
    )
    gram_term = gram_term.reshape(leaf_count, rank_size * rank_size)
    leaf_gram = lax.psum_scatter(gram_term, "samp", scatter_dimension=1, tiled=True)
    inner = inner_transfer.astype(jnp.float32).reshape(-1, rank_size, rank_size)
    current = cluster_coefficient_array
    offset = 0
    width_now = leaf_count
    while width_now > 1:
        mats = inner[offset : offset + width_now]
        projected = jnp.einsum("nab,nas->nbs", mats, current, precision=lax.Precision.HIGHEST)
        projected = projected.reshape(width_now // 2, 2, rank_size, column_count)
        current = projected[:, 0] + projected[:, 1]
        offset = offset + width_now
        width_now = width_now // 2
    accum = current[0]
    upper = upper_transfer.astype(jnp.float32).reshape(-1, rank_size, rank_size)
    group_total = lax.axis_size("leaf")
    heights = group_total.bit_length() - 1
    offset = 0
    width_now = group_total
    levels = []
    for height in range(heights):
        node_index = offset + jnp.right_shift(device, height)
        matrix = lax.dynamic_index_in_dim(upper, node_index, 0, keepdims=False)
        own_part = jnp.dot(matrix.T, accum, precision=lax.Precision.HIGHEST)
        accum = own_part + partner(own_part, "leaf", height)
        levels.append(accum)
        offset = offset + width_now
        width_now = width_now // 2
    ancestor_coeffs = jnp.stack(levels, axis=0)[None]
    return (cluster_coefficient_array, leaf_gram, ancestor_coeffs)


def solution(mesh):
    return jax.shard_map(
        shards,
        mesh=mesh,
        in_specs=(
            P("leaf", "samp"),
            P("leaf", "samp"),
            P("leaf", None, None),
            P("leaf", None, None, None),
            P("leaf", None),
            P("leaf"),
            P("leaf", None),
            P(),
        ),
        out_specs=(P("leaf", None, "samp"), P("leaf", "samp"), P("leaf", None, None, "samp")),
        check_vma=False,
    )
```

profile of v0, /device:TPU:0, one launch (start us, length us, event | category | flops | bytes accessed | tf_op | source)
XLA Modules:
  0.0 84.4 jit_solution(4635719382655436121)
XLA Ops:
  7.2 0.0 copy-start
  7.2 0.0 reduce-scatter.2.cloned.1.call-start
  7.2 1.4 %collective-permute-start.1 = (bf16[4096,64]{0,1:T(8,128)(2,1)}, bf16[4096,64]{0,1:T(8,128)(2,1)S(1)}, u32[]{:S(2)}, u32[]{:S(2)}) collective-permute-start(bf16[4096,64]{0,1:T(8,128)(2,1)} %param.9), channel_id=1, source_target_pairs={{4,0},{8,4},{12,8},{16,12},{20,16},{24,20},{28,24},{5,1},{9,5},{13... | collective-permute-start | bytes 1572872 | tf_op jit(solution)/shard_map/ppermute | solution.py:17
  8.7 6.3 %collective-permute-start = (bf16[4096,64]{0,1:T(8,128)(2,1)}, bf16[4096,64]{0,1:T(8,128)(2,1)}, u32[]{:S(2)}, u32[]{:S(2)}) collective-permute-start(bf16[4096,64]{0,1:T(8,128)(2,1)} %param.9), channel_id=1, source_target_pairs={{0,4},{4,8},{8,12},{12,16},{16,20},{20,24},{24,28},{1,5},{5,9},{9,... | collective-permute-start | bytes 1572872 | tf_op jit(solution)/shard_map/ppermute | solution.py:15
  15.0 0.9 %slice.76 = bf16[2,4096]{1,0:T(2,128)(2,1)S(1)} slice(bf16[62,4096]{1,0:T(8,128)(2,1)} %param.14), slice={[60:62], [0:4096]} | slice | bytes 32768 | tf_op jit(solution)/shard_map/slice | solution.py:69
  15.8 0.9 %slice.72 = bf16[4,4096]{1,0:T(4,128)(2,1)S(1)} slice(bf16[62,4096]{1,0:T(8,128)(2,1)} %param.14), slice={[56:60], [0:4096]} | slice | bytes 65536 | tf_op jit(solution)/shard_map/slice | solution.py:69
  16.7 0.8 %slice.68 = bf16[8,4096]{1,0:T(8,128)(2,1)S(1)} slice(bf16[62,4096]{1,0:T(8,128)(2,1)} %param.14), slice={[48:56], [0:4096]} | slice | bytes 131072 | tf_op jit(solution)/shard_map/slice | solution.py:69
  17.5 0.9 %slice.64 = bf16[16,4096]{1,0:T(8,128)(2,1)S(1)} slice(bf16[62,4096]{1,0:T(8,128)(2,1)} %param.14), slice={[32:48], [0:4096]} | slice | bytes 262144 | tf_op jit(solution)/shard_map/slice | solution.py:69
  18.4 1.0 %slice.60 = bf16[32,4096]{1,0:T(8,128)(2,1)S(1)} slice(bf16[62,4096]{1,0:T(8,128)(2,1)} %param.14), slice={[0:32], [0:4096]} | slice | bytes 524288 | tf_op jit(solution)/shard_map/slice | solution.py:69
  19.4 0.7 compare_select_fusion
  20.1 0.1 copy.46
  20.2 0.1 reshape.84
  20.3 1.8 %reshape.75 = bf16[14,64,64]{2,1,0:T(8,128)(2,1)} reshape(bf16[14,4096]{1,0:T(8,128)(2,1)} %param.15) | data formatting | bytes 229376 | tf_op jit(solution)/shard_map/reshape | solution.py:76
  22.1 0.7 slice.77
  22.9 0.8 slice.73
  23.6 0.2 slice.69
  23.8 0.2 slice.65
  24.0 0.5 slice.61
  24.6 0.7 fusion.44
  25.3 0.0 collective-permute-done.1
  25.3 10.5 %collective-permute-done = bf16[4096,64]{0,1:T(8,128)(2,1)} collective-permute-done((bf16[4096,64]{0,1:T(8,128)(2,1)}, bf16[4096,64]{0,1:T(8,128)(2,1)}, u32[]{:S(2)}, u32[]{:S(2)}) %collective-permute-start) | collective-permute-done | bytes 524320 | tf_op jit(solution)/shard_map/ppermute | solution.py:15
  35.9 1.6 %copy_bitcast_fusion = bf16[96,128,64]{1,2,0:T(8,128)(2,1)S(1)} fusion(bf16[4096,64]{0,1:T(8,128)(2,1)S(1)} %collective-permute-done.1, bf16[4096,64]{0,1:T(8,128)(2,1)} %param.9, bf16[4096,64]{0,1:T(8,128)(2,1)} %collective-permute-done), kind=kLoop, calls=%fused_computation.4 | loop fusion | flops 4718592 | bytes 3145728 | tf_op jit(solution)/shard_map/reshape | solution.py:37
  37.5 0.0 copy-start.3
  37.5 3.0 %gather_fusion = bf16[256,128,64]{1,2,0:T(8,128)(2,1)} fusion(bf16[96,128,64]{1,2,0:T(8,128)(2,1)S(1)} %copy_bitcast_fusion, s32[1024]{0:T(1024)S(1)} %pad_clamp_fusion), kind=kCustom, calls=%fused_computation | custom fusion | bytes 8389632 | tf_op jit(solution)/shard_map/gather | solution.py:41
  40.6 0.0 copy-done
  40.6 0.0 copy-done.3
  40.6 6.4 %fusion.13 = f32[32,64,64]{2,1,0:T(8,128)S(1)} fusion(bf16[32,64,128]{2,1,0:T(8,128)(2,1)S(1)} %copy-done, bf16[32,8,128,128]{3,2,1,0:T(8,128)(2,1)} %param.11, bf16[32,8,128,64]{2,3,1,0:T(8,128)(2,1)} %bitcast.133, bf16[32,8]{1,0:T(8,128)(2,1)S(1)} %fusion.44, bf16[4096,64]{0,1:T(8,128)(2,1)S(1)} %copy-done.3), kind=kOutput, calls=%fused_computation.10 | convolution fusion | flops 573308928 | bytes 14156288 | tf_op jit(solution)/shard_map/grb,gbs->grs/dot_general | solution.py:49
  47.0 0.0 copy-start.1
  47.0 0.0 copy-start.2
  47.0 0.6 fusion.50
  47.6 0.4 fusion.19
  48.0 0.3 fusion.23
  48.3 0.0 copy-done.1
  48.3 0.2 fusion.27
  48.5 0.0 copy-done.2
  48.5 0.2 convolution_bitcast_fusion
  48.7 0.9 %fusion.33 = f32[64,64]{1,0:T(8,128)S(1)} fusion(f32[1,2,64,64]{2,3,1,0:T(8,128)S(1)} %convolution_bitcast_fusion, bf16[14,64,64]{2,1,0:T(8,128)(2,1)} %reshape.75, s32[]{:T(128)S(6)} %select_n.14), kind=kOutput, calls=%fused_computation.37 | convolution fusion | flops 3149824 | bytes 65540 | tf_op jit(solution)/shard_map/dot_general | solution.py:85
  49.6 2.5 %collective-permute-start.2 = (f32[64,64]{1,0:T(8,128)S(1)}, f32[64,64]{1,0:T(8,128)S(1)}, u32[]{:S(2)}, u32[]{:S(2)}) collective-permute-start(f32[64,64]{1,0:T(8,128)S(1)} %fusion.33), channel_id=1, source_target_pairs={{0,4},{4,0},{8,12},{12,8},{16,20},{20,16},{24,28},{28,24},{1,5},{5... | collective-permute-start | bytes 49160 | tf_op jit(solution)/shard_map/ppermute | solution.py:25
  52.2 1.8 %convolution_multiply_fusion = f32[32,64,64]{2,1,0:T(8,128)S(1)} fusion(f32[32,64,64]{2,1,0:T(8,128)S(1)} %fusion.13), kind=kOutput, calls=%fused_computation.7 | convolution fusion | flops 100794368 | bytes 1048576 | tf_op jit(solution)/shard_map/ydb,ykb->ydk/dot_general | solution.py:54
  54.0 1.3 %copy.58 = f32[32,64,64]{2,1,0:T(8,128)} copy(f32[32,64,64]{1,2,0:T(8,128)S(1)} %bitcast.134) | data formatting | bytes 1048576
  55.3 1.2 %reshape.74 = f32[32,4096]{1,0:T(8,128)} reshape(f32[32,64,64]{2,1,0:T(8,128)S(1)} %convolution_multiply_fusion) | data formatting | bytes 1048576 | tf_op jit(solution)/shard_map/reshape | solution.py:62
  56.5 0.0 reduce-scatter.2.cloned.1.call-update
  56.5 0.0 collective-permute-done.2
  56.5 0.9 %fusion.38 = f32[64,64]{1,0:T(8,128)S(1)} fusion(bf16[14,64,64]{2,1,0:T(8,128)(2,1)} %reshape.75, s32[]{:T(128)S(6)} %select_n.15, f32[64,64]{1,0:T(8,128)S(1)} %fusion.33, f32[64,64]{1,0:T(8,128)S(1)} %collective-permute-done.2), kind=kOutput, calls=%fused_computation.42 | convolution fusion | flops 3149824 | bytes 65540 | tf_op jit(solution)/shard_map/dot_general | solution.py:85
  57.4 1.6 %collective-permute-start.3 = (f32[64,64]{1,0:T(8,128)S(1)}, f32[64,64]{1,0:T(8,128)S(1)}, u32[]{:S(2)}, u32[]{:S(2)}) collective-permute-start(f32[64,64]{1,0:T(8,128)S(1)} %fusion.38), channel_id=1, source_target_pairs={{0,8},{4,12},{8,0},{12,4},{16,24},{20,28},{24,16},{28,20},{1,9},{5... | collective-permute-start | bytes 49160 | tf_op jit(solution)/shard_map/ppermute | solution.py:25
  59.1 2.3 %collective-permute-done.3 = f32[64,64]{1,0:T(8,128)S(1)} collective-permute-done((f32[64,64]{1,0:T(8,128)S(1)}, f32[64,64]{1,0:T(8,128)S(1)}, u32[]{:S(2)}, u32[]{:S(2)}) %collective-permute-start.3) | collective-permute-done | bytes 16416 | tf_op jit(solution)/shard_map/ppermute | solution.py:25
  61.4 0.9 %fusion.36 = f32[64,64]{1,0:T(8,128)S(1)} fusion(bf16[14,64,64]{2,1,0:T(8,128)(2,1)} %reshape.75, s32[]{:T(128)S(6)} %select_n.16, f32[64,64]{1,0:T(8,128)S(1)} %fusion.38, f32[64,64]{1,0:T(8,128)S(1)} %collective-permute-done.3), kind=kOutput, calls=%fused_computation.40 | convolution fusion | flops 3149824 | bytes 65540 | tf_op jit(solution)/shard_map/dot_general | solution.py:85
  62.3 2.7 %collective-permute-start.4 = (f32[64,64]{1,0:T(8,128)S(1)}, f32[64,64]{1,0:T(8,128)S(1)}, u32[]{:S(2)}, u32[]{:S(2)}) collective-permute-start(f32[64,64]{1,0:T(8,128)S(1)} %fusion.36), channel_id=1, source_target_pairs={{0,16},{4,20},{8,24},{12,28},{16,0},{20,4},{24,8},{28,12},{1,17},{... | collective-permute-start | bytes 49160 | tf_op jit(solution)/shard_map/ppermute | solution.py:25
  65.0 2.2 %collective-permute-done.4 = f32[64,64]{1,0:T(8,128)S(1)} collective-permute-done((f32[64,64]{1,0:T(8,128)S(1)}, f32[64,64]{1,0:T(8,128)S(1)}, u32[]{:S(2)}, u32[]{:S(2)}) %collective-permute-start.4) | collective-permute-done | bytes 16416 | tf_op jit(solution)/shard_map/ppermute | solution.py:25
  67.2 0.7 maximum_bitcast_fusion.1
  67.9 9.7 %reduce-scatter.2.cloned.1.call-done = f32[32,1024]{1,0:T(8,128)} async-done(((f32[32,4096]{1,0:T(8,128)}), f32[32,1024]{1,0:T(8,128)}) %reduce-scatter.2.cloned.1.call-update) | async-done | bytes 131088 | tf_op jit(solution)/shard_map/reduce_scatter | solution.py:63
  (4 shorter events, 0.0 us)
Async XLA Ops:
  7.2 33.4 %copy-start = (bf16[32,64,128]{2,1,0:T(8,128)(2,1)S(1)}, bf16[32,64,128]{2,1,0:T(8,128)(2,1)}, u32[]{:S(2)}) copy-start(bf16[32,64,128]{2,1,0:T(8,128)(2,1)} %param.10) | copy-start | bytes 1572868
  7.2 70.4 %reduce-scatter.2.cloned.1.call-start = ((), (), s32[]{:S(2)}) async-start(), calls=%async_computation.1 | async-start | bytes 655360 | tf_op jit(solution)/shard_map/reduce_scatter | solution.py:63
  7.2 18.1 %collective-permute-start.1 = (bf16[4096,64]{0,1:T(8,128)(2,1)}, bf16[4096,64]{0,1:T(8,128)(2,1)S(1)}, u32[]{:S(2)}, u32[]{:S(2)}) collective-permute-start(bf16[4096,64]{0,1:T(8,128)(2,1)} %param.9), channel_id=1, source_target_pairs={{4,0},{8,4},{12,8},{16,12},{20,16},{24,20},{28,24},{5,1},{9,5},{13... | collective-permute-start | bytes 1572872 | tf_op jit(solution)/shard_map/ppermute | solution.py:17
  8.7 27.2 %collective-permute-start = (bf16[4096,64]{0,1:T(8,128)(2,1)}, bf16[4096,64]{0,1:T(8,128)(2,1)}, u32[]{:S(2)}, u32[]{:S(2)}) collective-permute-start(bf16[4096,64]{0,1:T(8,128)(2,1)} %param.9), channel_id=1, source_target_pairs={{0,4},{4,8},{8,12},{12,16},{16,20},{20,24},{24,28},{1,5},{5,9},{9,... | collective-permute-start | bytes 1572872 | tf_op jit(solution)/shard_map/ppermute | solution.py:15
  37.5 3.1 %copy-start.3 = (bf16[4096,64]{0,1:T(8,128)(2,1)S(1)}, bf16[4096,64]{0,1:T(8,128)(2,1)}, u32[]{:S(2)}) copy-start(bf16[4096,64]{0,1:T(8,128)(2,1)} %param.8) | copy-start | bytes 1572868
  47.0 1.3 %copy-start.1 = (bf16[4,64,64]{2,1,0:T(8,128)(2,1)S(1)}, bf16[4,64,64]{2,1,0:T(8,128)(2,1)}, u32[]{:S(2)}) copy-start(bf16[4,64,64]{2,1,0:T(8,128)(2,1)} %slice.73) | copy-start | bytes 98308
  47.0 1.5 %copy-start.2 = (bf16[2,64,64]{2,1,0:T(8,128)(2,1)S(1)}, bf16[2,64,64]{2,1,0:T(8,128)(2,1)}, u32[]{:S(2)}) copy-start(bf16[2,64,64]{2,1,0:T(8,128)(2,1)} %slice.77) | copy-start | bytes 49156
  49.6 6.9 %collective-permute-start.2 = (f32[64,64]{1,0:T(8,128)S(1)}, f32[64,64]{1,0:T(8,128)S(1)}, u32[]{:S(2)}, u32[]{:S(2)}) collective-permute-start(f32[64,64]{1,0:T(8,128)S(1)} %fusion.33), channel_id=1, source_target_pairs={{0,4},{4,0},{8,12},{12,8},{16,20},{20,16},{24,28},{28,24},{1,5},{5... | collective-permute-start | bytes 49160 | tf_op jit(solution)/shard_map/ppermute | solution.py:25
  57.4 4.0 %collective-permute-start.3 = (f32[64,64]{1,0:T(8,128)S(1)}, f32[64,64]{1,0:T(8,128)S(1)}, u32[]{:S(2)}, u32[]{:S(2)}) collective-permute-start(f32[64,64]{1,0:T(8,128)S(1)} %fusion.38), channel_id=1, source_target_pairs={{0,8},{4,12},{8,0},{12,4},{16,24},{20,28},{24,16},{28,20},{1,9},{5... | collective-permute-start | bytes 49160 | tf_op jit(solution)/shard_map/ppermute | solution.py:25
  62.3 4.9 %collective-permute-start.4 = (f32[64,64]{1,0:T(8,128)S(1)}, f32[64,64]{1,0:T(8,128)S(1)}, u32[]{:S(2)}, u32[]{:S(2)}) collective-permute-start(f32[64,64]{1,0:T(8,128)S(1)} %fusion.36), channel_id=1, source_target_pairs={{0,16},{4,20},{8,24},{12,28},{16,0},{20,4},{24,8},{28,12},{1,17},{... | collective-permute-start | bytes 49160 | tf_op jit(solution)/shard_map/ppermute | solution.py:25
Sparse Core Ops, SparseCore 0:
  56.6 20.9 reduce-scatter.1
where the time goes:
time: 85 us; the launch traced here: 84.4 us
  waiting for transfers between devices  24.8 us (29%)
  starting transfers between devices  14.6 us (17%)
  local copies, waits for them, and re-layouts  14.4 us (17%)
  between operations  14.2 us (17%)
  matrix products  12.6 us (15%)
  other arithmetic  3.73 us (4%)
    ppermute x1, waiting for transfers between devices, with_halo(): lax.ppermute(tail, axis, [(i, (i + 1) % count) for i in range(ends)])  10.5 us
    reduce_scatter x1, waiting for transfers between devices, shards(): lax.psum_scatter(gram_term, 'samp', scatter_dimension=1, tiled=True)  9.7 us
    slice x10, local copies, waits for them, and re-layouts, shards(): mats = inner[offset:offset + width_now]  6.86 us
    ppermute x3, starting transfers between devices, partner(): lax.ppermute(shard, axis, [(i, i ^ 1 << stride) for i in range(lax.axis_s...  6.84 us
    dot_general x1, matrix products, shards(): jnp.einsum('grb,gbs->grs', leaf_basis, far_part, preferred_element_type=j...  6.4 us
    ppermute x1, starting transfers between devices, with_halo(): lax.ppermute(tail, axis, [(i, (i + 1) % count) for i in range(ends)])  6.31 us
    ppermute x3, waiting for transfers between devices, partner(): lax.ppermute(shard, axis, [(i, i ^ 1 << stride) for i in range(lax.axis_s...  4.55 us
    gather x1, local copies, waits for them, and re-layouts, shards(): fetched = widened[local_index]  3.04 us
  transfers between devices with their start and end apart: 6, of which 4 were waited for; matrix products, arithmetic and copies ran while one was open for 20% of the time, Pallas kernels for 0%

commit v1 on v0

v1 whole, which is shorter than its diff:
```python
import functools

import jax
import jax.numpy as jnp
from jax import lax
from jax.experimental import pallas as pl
from jax.experimental.pallas import tpu as pltpu
from jax.sharding import PartitionSpec as P

MESH = pl.DeviceIdType.MESH
F32 = jnp.float32
BF16 = jnp.bfloat16


def split(x):
    high = x.astype(BF16)
    return high, (x - high.astype(F32)).astype(BF16)


def dot_nt(a, b):
    return lax.dot_general(a, b, (((1,), (1,)), ((), ())), preferred_element_type=F32)


def dot(a, b):
    return jnp.dot(a, b, preferred_element_type=F32)


def chain_step(rows, mats):
    high, low = split(rows)
    n = rows.shape[0]
    both = dot_nt(jnp.concatenate([high, low], axis=0), mats)
    return both[:n] + both[n:]


def kernel(
    n_leaf, n_samp, total_columns,
    index_ref, count_ref, inner_ref, upper_ref, omega_hbm, samples_hbm, basis_hbm, near_hbm,
    coeff_hbm, gram_ref, ancestor_ref,
    omega_v, samples_v, basis_v, near_v, own, land_l, land_r, held, packed,
    inner_v, upper_v, paths, leaf_high, leaf_low, up_acc, up_send, up_recv,
    gram_send, gram_recv, gram_sum, gram_mix, coeff_v,
    load_sem, near_sem, send_l, send_r, recv_l, recv_r,
    gram_ssem, gram_rsem, up_ssem, up_rsem, out_sem,
):
    leaf = lax.axis_index("leaf")
    samp = lax.axis_index("samp")
    leaf_count, rank, leaf_size = basis_v.shape
    slots = near_v.shape[1]
    width = omega_v.shape[0]
    pairs = leaf_count // 2
    half = pairs // 2
    heights = ancestor_ref.shape[0]
    chunk = 2
    steps = half // chunk
    part = rank // n_samp
    nodes = inner_ref.shape[0]

    load_omega = pltpu.make_async_copy(omega_hbm, omega_v, load_sem.at[0])
    load_samples = pltpu.make_async_copy(samples_hbm, samples_v, load_sem.at[1])
    load_basis = pltpu.make_async_copy(basis_hbm, basis_v, load_sem.at[2])
    load_near = pltpu.make_async_copy(near_hbm, near_v, near_sem)
    load_omega.start()
    load_samples.start()
    load_basis.start()
    load_near.start()

    barrier = pltpu.get_barrier_semaphore()
    for d in range(1, n_leaf):
        pl.semaphore_signal(barrier, inc=1, device_id=(leaf ^ d, samp), device_id_type=MESH)
    for d in range(1, n_samp):
        pl.semaphore_signal(barrier, inc=1, device_id=(leaf, samp ^ d), device_id_type=MESH)

    load_omega.wait()

    def pair_tile(src, u):
        at = pl.multiple_of(u * 2 * leaf_size, 2 * leaf_size)
        rows = jnp.concatenate(
            [src[:, pl.ds(at, leaf_size)], src[:, pl.ds(at + leaf_size, leaf_size)]], axis=0
        )
        return rows.T

    def pack_omega(u, carry):
        tile = pair_tile(omega_v, u)
        own[u] = tile
        held[pairs + u] = tile
        return carry

    lax.fori_loop(0, pairs, pack_omega, 0)
    pl.semaphore_wait(barrier, n_leaf + n_samp - 2)

    def to_right(c):
        lo, size = (half, half) if c == 0 else (half - chunk * c, chunk)
        return pltpu.make_async_remote_copy(
            src_ref=own.at[pl.ds(lo, size)], dst_ref=land_l.at[pl.ds(lo, size)],
            send_sem=send_r.at[c], recv_sem=recv_l.at[c],
            device_id=(leaf + 1, samp), device_id_type=MESH,
        )

    def to_left(c):
        lo, size = (0, half) if c == 0 else (half + chunk * (c - 1), chunk)
        return pltpu.make_async_remote_copy(
            src_ref=own.at[pl.ds(lo, size)], dst_ref=land_r.at[pl.ds(lo, size)],
            send_sem=send_l.at[c], recv_sem=recv_r.at[c],
            device_id=(leaf - 1, samp), device_id_type=MESH,
        )

    for c in range(steps + 1):
        @pl.when(leaf < n_leaf - 1)
        def _():
            to_right(c).start()

        @pl.when(leaf > 0)
        def _():
            to_left(c).start()

    for r in range(rank * rank // 128):
        for src, dst in ((inner_ref, inner_v), (upper_ref, upper_v)):
            count = src.shape[0]
            tile = src[:, 128 * r:128 * r + 128].astype(F32)
            dst[pl.ds(2 * r, count, stride=rank), :] = tile
            dst[pl.ds(2 * r + 1, count, stride=rank), :] = pltpu.roll(tile, 64, 1)

    eye = (
        lax.broadcasted_iota(jnp.int32, (rank, rank), 0)
        == lax.broadcasted_iota(jnp.int32, (rank, rank), 1)
    ).astype(F32)
    rows = None
    starts = []
    offset = 0
    for h in range(heights):
        starts.append(offset)
        offset += n_leaf >> h
    for h in reversed(range(heights)):
        node = starts[h] + lax.shift_right_logical(leaf, h)
        mat = upper_v[pl.ds(pl.multiple_of(node * rank, rank), rank), :][:, :rank].astype(BF16)
        rows = eye if rows is None else jnp.concatenate([eye, rows], axis=0)
        rows = chain_step(rows, mat)
    paths[nodes] = rows

    def children(q):
        mats = inner_v[pl.ds(pl.multiple_of(q * 2 * rank, 2 * rank), 2 * rank), :]
        return chain_step(paths[leaf_count + q], mats[:, :rank].astype(BF16))

    def inner_pair(i, carry):
        q = leaf_count - 2 - i
        both = children(q)
        paths[2 * q] = both[:, :rank]
        paths[2 * q + 1] = pltpu.roll(both, 64, 1)[:, :rank]
        return carry

    lax.fori_loop(0, pairs - 1, inner_pair, 0)

    def leaf_pair(q, carry):
        high, low = split(children(q))
        leaf_high[q] = high
        leaf_low[q] = low
        return carry

    lax.fori_loop(0, pairs, leaf_pair, 0)

    load_samples.wait()

    def pack_samples(u, carry):
        packed[u] = pair_tile(samples_v, u)
        return carry

    lax.fori_loop(0, pairs, pack_samples, 0)
    up_acc[...] = jnp.zeros_like(up_acc)
    load_basis.wait()
    load_near.wait()

    lane_half = lax.broadcasted_iota(jnp.int32, (1, 128), 1) // 64
    lower = lax.broadcasted_iota(jnp.int32, (leaf_size, 128), 1) < 64
    base = leaf * leaf_count - leaf_count

    def near_product(p):
        tiles = []
        for k in range(slots):
            at = jnp.clip(index_ref[k, p] - base, 0, 3 * leaf_count - 1)
            want = jnp.where(k < count_ref[p], at % 2, 2)
            mask = (lane_half == want).astype(F32).astype(BF16)
            tiles.append(held[at // 2] * mask)
        left = jnp.concatenate([near_v[p, k] for k in range(slots)], axis=1)
        total = dot(left, jnp.concatenate(tiles, axis=0))
        return total + pltpu.roll(total, 64, 1)

    def process(u, w):
        near = jnp.where(lower, near_product(2 * u), near_product(2 * u + 1))
        far = (packed[u].astype(F32) - near).astype(BF16)
        basis = basis_v[pl.ds(2 * u, 2)].reshape(2 * rank, leaf_size)
        both = dot(basis, far)
        top, bottom = both[:rank], both[rank:]
        coeff_v[2 * u] = top[:, :width]
        coeff_v[2 * u + 1] = pltpu.roll(bottom, 64, 1)[:, :width]
        low_lane = lower[:rank]
        top = jnp.where(low_lane, top, 0.0)
        bottom = jnp.where(low_lane, 0.0, bottom)
        top_high, top_low = split(top)
        bottom_high, bottom_low = split(bottom)
        block_high = jnp.concatenate([top_high, bottom_high], axis=0)
        block_low = jnp.concatenate([top_low, bottom_low], axis=0)
        row_high = top_high + bottom_high
        row_low = top_low + bottom_low
        gram = dot_nt(
            jnp.concatenate([row_high, row_high, row_low], axis=1),
            jnp.concatenate([block_high, block_low, block_high], axis=1),
        ) * (1.0 / total_columns)
        for t in range(n_samp):
            gram_send[t, pl.ds(pl.multiple_of(w * part, part), part), :] = (
                gram[t * part:(t + 1) * part].astype(gram_send.dtype)
            )
        path_high, path_low = leaf_high[u], leaf_low[u]
        up_acc[...] += dot(
            jnp.concatenate([path_high, path_high, path_low], axis=1),
            jnp.concatenate([block_high, block_low, block_high], axis=0),
        )

    def accept(land, at_held, lo, size):
        def body(i, carry):
            held[at_held + lo + i] = land[lo + i]
            return carry

        lax.fori_loop(0, size, body, 0)

    @pl.when(leaf > 0)
    def _():
        to_right(0).wait_recv()
        accept(land_l, 0, half, half)

    @pl.when(leaf < n_leaf - 1)
    def _():
        to_left(0).wait_recv()
        accept(land_r, 2 * pairs, 0, half)

    span = 2 * chunk * part

    def gram_copy(d, j):
        at = pl.ds(pl.multiple_of(j * span, span), span)
        return pltpu.make_async_remote_copy(
            src_ref=gram_send.at[samp ^ d, at], dst_ref=gram_recv.at[d - 1, at],
            send_sem=gram_ssem.at[d - 1, j], recv_sem=gram_rsem.at[d - 1, j],
            device_id=(leaf, samp ^ d), device_id_type=MESH,
        )

    def out_copy(j, side):
        lo = 2 * (half - chunk * (j + 1)) if side == 0 else 2 * (half + chunk * j)
        at = pl.ds(lo, 2 * chunk)
        return pltpu.make_async_copy(coeff_v.at[at], coeff_hbm.at[at], out_sem.at[side, j])

    for j in range(steps):
        lo_l = half - chunk * (j + 1)
        lo_r = half + chunk * j

        @pl.when(leaf > 0)
        def _():
            to_right(j + 1).wait_recv()
            accept(land_l, 0, lo_l, chunk)

        @pl.when(leaf < n_leaf - 1)
        def _():
            to_left(j + 1).wait_recv()
            accept(land_r, 2 * pairs, lo_r, chunk)

        def body(i, carry):
            process(lo_l + i, 2 * chunk * j + i)
            process(lo_r + i, 2 * chunk * j + chunk + i)
            return carry

        lax.fori_loop(0, chunk, body, 0)
        for d in range(1, n_samp):
            gram_copy(d, j).start()
        out_copy(j, 0).start()
        out_copy(j, 1).start()

    total = up_acc[...]
    total = total + pltpu.roll(total, 64, 1)
    side = rank // 2
    for h in range(heights):
        up_send[h * side:(h + 1) * side] = jnp.where(
            lower[:side], total[h * rank:h * rank + side], total[h * rank + side:(h + 1) * rank]
        )

    def up_copy(d):
        first = (d.bit_length() - 1) * side
        at = pl.ds(first, heights * side - first)
        return pltpu.make_async_remote_copy(
            src_ref=up_send.at[at], dst_ref=up_recv.at[d - 1, at],
            send_sem=up_ssem.at[d - 1], recv_sem=up_rsem.at[d - 1],
            device_id=(leaf ^ d, samp), device_id_type=MESH,
        )

    for d in range(1, n_leaf):
        up_copy(d).start()

    for j in range(steps):
        for d in range(1, n_samp):
            gram_copy(d, j).wait_recv()
    for w in range(pairs):
        j, i = divmod(w, 2 * chunk)
        u = half - chunk * (j + 1) + i if i < chunk else half + chunk * j + i - chunk
        at = slice(w * part, (w + 1) * part)
        value = gram_send[samp, at, :].astype(F32)
        for d in range(1, n_samp):
            value = value + gram_recv[d - 1, at, :].astype(F32)
        gram_sum[u * part:(u + 1) * part, :] = value
    low16 = lower[:pairs]
    for m in range(part // 2):
        first = gram_sum[pl.ds(2 * m, pairs, stride=part), :]
        second = gram_sum[pl.ds(2 * m + 1, pairs, stride=part), :]
        even = jnp.where(low16, first, pltpu.roll(second, 64, 1))
        odd = jnp.where(low16, pltpu.roll(first, 64, 1), second)
        lo = m * leaf_count
        gram_mix[pl.ds(lo, pairs, stride=2), :] = even
        gram_mix[pl.ds(lo + 1, pairs, stride=2), :] = odd
        gram_ref[:, 128 * m:128 * m + 128] = gram_mix[lo:lo + leaf_count, :]

    for d in range(1, n_leaf):
        up_copy(d).wait_recv()
    for h in range(heights):
        at = slice(h * side, (h + 1) * side)
        value = up_send[at, :]
        for d in range(1, n_leaf):
            if d.bit_length() <= h + 1:
                value = value + up_recv[d - 1, at, :]
        ancestor_ref[h, 0:side, :] = value[:, :width]
        ancestor_ref[h, side:rank, :] = pltpu.roll(value, 64, 1)[:, :width]

    for c in range(steps + 1):
        @pl.when(leaf < n_leaf - 1)
        def _():
            to_right(c).wait_send()

        @pl.when(leaf > 0)
        def _():
            to_left(c).wait_send()

    for j in range(steps):
        for d in range(1, n_samp):
            gram_copy(d, j).wait_send()
        out_copy(j, 0).wait()
        out_copy(j, 1).wait()
    for d in range(1, n_leaf):
        up_copy(d).wait_send()


def shards(
    n_leaf, n_samp,
    samples, omega, leaf_basis, near_blocks, near_index, near_count, inner_transfer, upper_transfer
):
    leaf_count, rank, leaf_size = leaf_basis.shape
    width = samples.shape[1]
    pairs = leaf_count // 2
    steps = pairs // 4
    heights = n_leaf.bit_length() - 1
    part = rank // n_samp
    nodes = inner_transfer.shape[0]
    upper_nodes = upper_transfer.shape[0]
    wire = BF16 if part % 16 == 0 else F32
    omega, samples, near_index = omega.T, samples.T, near_index.T
    vmem = pl.BlockSpec(memory_space=pltpu.VMEM)
    smem = pl.BlockSpec(memory_space=pltpu.SMEM)
    hbm = pl.BlockSpec(memory_space=pl.ANY)
    dma = pltpu.SemaphoreType.DMA
    coeffs, gram, ancestors = pl.pallas_call(
        functools.partial(kernel, n_leaf, n_samp, width * n_samp),
        out_shape=(
            jax.ShapeDtypeStruct((leaf_count, rank, width), F32),
            jax.ShapeDtypeStruct((leaf_count, part * rank), F32),
            jax.ShapeDtypeStruct((heights, rank, width), F32),
        ),
        in_specs=[smem, smem, vmem, vmem, hbm, hbm, hbm, hbm],
        out_specs=(hbm, vmem, vmem),
        scratch_shapes=[
            pltpu.VMEM(omega.shape, BF16),
            pltpu.VMEM(samples.shape, BF16),
            pltpu.VMEM(leaf_basis.shape, BF16),
            pltpu.VMEM(near_blocks.shape, BF16),
            pltpu.VMEM((pairs, leaf_size, 128), BF16),
            pltpu.VMEM((pairs, leaf_size, 128), BF16),
            pltpu.VMEM((pairs, leaf_size, 128), BF16),
            pltpu.VMEM((3 * pairs, leaf_size, 128), BF16),
            pltpu.VMEM((pairs, leaf_size, 128), BF16),
            pltpu.VMEM((nodes * rank, 128), F32),
            pltpu.VMEM((upper_nodes * rank, 128), F32),
            pltpu.VMEM((nodes + 1, heights * rank, rank), F32),
            pltpu.VMEM((pairs, heights * rank, 128), BF16),
            pltpu.VMEM((pairs, heights * rank, 128), BF16),
            pltpu.VMEM((heights * rank, 128), F32),
            pltpu.VMEM((heights * rank // 2, 128), F32),
            pltpu.VMEM((n_leaf - 1, heights * rank // 2, 128), F32),
            pltpu.VMEM((n_samp, pairs * part, 128), wire),
            pltpu.VMEM((n_samp - 1, pairs * part, 128), wire),
            pltpu.VMEM((pairs * part, 128), F32),
            pltpu.VMEM((part // 2 * leaf_count, 128), F32),
            pltpu.VMEM((leaf_count, rank, width), F32),
            dma((3,)), dma,
            dma((steps + 1,)), dma((steps + 1,)), dma((steps + 1,)), dma((steps + 1,)),
            dma((n_samp - 1, steps)), dma((n_samp - 1, steps)),
            dma((n_leaf - 1,)), dma((n_leaf - 1,)),
            dma((2, steps)),
        ],
        compiler_params=pltpu.CompilerParams(
            collective_id=0, has_side_effects=True, vmem_limit_bytes=56 * 1024 * 1024
        ),
    )(near_index, near_count, inner_transfer, upper_transfer, omega, samples, leaf_basis, near_blocks)
    return coeffs, gram, ancestors[None]


def solution(mesh):
    return jax.shard_map(
        functools.partial(shards, mesh.shape["leaf"], mesh.shape["samp"]),
        mesh=mesh,
        in_specs=(
            P("leaf", "samp"),
            P("leaf", "samp"),
            P("leaf", None, None),
            P("leaf", None, None, None),
            P("leaf", None),
            P("leaf"),
            P("leaf", None),
            P(),
        ),
        out_specs=(P("leaf", None, "samp"), P("leaf", "samp"), P("leaf", None, None, "samp")),
        check_vma=False,
    )
```

time: 85 us -> 50.9 us (0.60)
  Pallas kernels: 0 us -> 44.6 us
  waiting for transfers between devices: 24.8 us -> 0 us
  starting transfers between devices: 14.6 us -> 0 us
  between operations: 14.2 us -> 0.64 us
  matrix products: 12.6 us -> 0 us
  local copies, waits for them, and re-layouts: 14.4 us -> 5.41 us
  other arithmetic: 3.73 us -> 0 us
    pallas_call x0 -> x1, Pallas kernels: none -> 44.6 us  [shards(): pl.pallas_call(functools.partial(kernel, n_leaf, n_samp, width * n_samp),...]
    ppermute x5 -> x0, waiting for transfers between devices: 15.1 us -> none  [the longest x1 10.5 us: with_halo(): lax.ppermute(tail, axis, [(i, (i + 1) % count) for i in range(ends)])]
    ppermute x5 -> x0, starting transfers between devices: 14.6 us -> none  [the longest x3 6.84 us: partner(): lax.ppermute(shard, axis, [(i, i ^ 1 << stride) for i in range(lax.axis_s...]
    dot_general x10 -> x0, matrix products: 12.6 us -> none  [the longest x1 6.4 us: shards(): jnp.einsum('grb,gbs->grs', leaf_basis, far_part, preferred_element_type=j...]
    reduce_scatter x1 -> x0, waiting for transfers between devices: 9.7 us -> none  [shards(): lax.psum_scatter(gram_term, 'samp', scatter_dimension=1, tiled=True)]
    slice x10 -> x0, local copies, waits for them, and re-layouts: 6.86 us -> none  [shards(): mats = inner[offset:offset + width_now]]
    unnamed x9 -> x3, local copies, waits for them, and re-layouts: 1.34 us -> 5.41 us
    gather x1 -> x0, local copies, waits for them, and re-layouts: 3.04 us -> none  [shards(): fetched = widened[local_index]]
  transfers between devices with their start and end apart: 6 -> 0, of which waited for: 4 -> 0; matrix products, arithmetic and copies ran while one was open for 20% -> 0% of each run, Pallas kernels for 0% -> 0%
where the time goes in v1:
time: 50.9 us; the launch traced here: 50.7 us
  Pallas kernels  44.6 us (88%)
  local copies, waits for them, and re-layouts  5.41 us (11%)
  between operations  0.64 us (1%)
    pallas_call x1, Pallas kernels, shards(): pl.pallas_call(functools.partial(kernel, n_leaf, n_samp, width * n_samp),...  44.6 us
    unnamed x3, local copies, waits for them, and re-layouts  5.41 us

profile of v1, /device:TPU:0, one launch (start us, length us, event | category | flops | bytes accessed | tf_op | source)
XLA Modules:
  0.0 50.7 jit_solution(2734117091490175266)
XLA Ops:
  0.6 44.6 %shard_map.103 = (f32[32,64,64]{2,1,0:T(8,128)}, f32[32,1024]{1,0:T(8,128)}, f32[3,64,64]{2,1,0:T(8,128)}) custom-call(s32[8,32]{1,0:T(8,128)} %bitcast.7, s32[32]{0:T(128)} %count_ref.1, bf16[62,4096]{1,0:T(8,128)(2,1)} %inner_ref.1, bf16[14,4096]{1,0:T(8,128)(2,1)} %upper_ref.1, bf16[64,4096]{1,0:T(8,128)(2,1)} %bitcast.4, bf16[64,4096]{1,0:T(8,128)(2,1)} %bitcast.5, ...), custom_call_target="tpu_custom_call" | custom-call | tf_op jit(solution)/shard_map/pallas_call | solution.py:364
  45.3 2.3 %copy.14 = f32[32,64,64]{2,1,0:T(8,128)} copy(f32[32,64,64]{2,1,0:T(8,128)} %get-tuple-element.12) | data formatting | bytes 1048576
  47.6 1.6 %copy.15 = f32[32,1024]{1,0:T(8,128)} copy(f32[32,1024]{1,0:T(8,128)} %get-tuple-element.13) | data formatting | bytes 262144
  49.1 1.5 %copy.16 = f32[1,3,64,64]{3,2,1,0:T(8,128)} copy(f32[1,3,64,64]{3,2,1,0:T(8,128)} %bitcast.6) | data formatting | bytes 98304

commit v2 on v1

--- a/solution.py
+++ b/solution.py
@@ -37,7 +37,7 @@
     index_ref, count_ref, inner_ref, upper_ref, omega_hbm, samples_hbm, basis_hbm, near_hbm,
     coeff_hbm, gram_ref, ancestor_ref,
     omega_v, samples_v, basis_v, near_v, own, land_l, land_r, held, packed,
-    inner_v, upper_v, paths, leaf_high, leaf_low, up_acc, up_send, up_recv,
+    inner_v, upper_v, paths, ascend, leaf_path, up_acc, up_send, up_recv,
     gram_send, gram_recv, gram_sum, gram_mix, coeff_v,
     load_sem, near_sem, send_l, send_r, recv_l, recv_r,
     gram_ssem, gram_rsem, up_ssem, up_rsem, out_sem,
@@ -50,8 +50,7 @@
     pairs = leaf_count // 2
     half = pairs // 2
     heights = ancestor_ref.shape[0]
-    chunk = 2
-    steps = half // chunk
+    steps = half
     part = rank // n_samp
     nodes = inner_ref.shape[0]
 
@@ -85,33 +84,43 @@
         held[pairs + u] = tile
         return carry
 
-    lax.fori_loop(0, pairs, pack_omega, 0)
+    lax.fori_loop(0, pairs, pack_omega, 0, unroll=4)
     pl.semaphore_wait(barrier, n_leaf + n_samp - 2)
 
-    def to_right(c):
-        lo, size = (half, half) if c == 0 else (half - chunk * c, chunk)
+    def to_right(c, lo, size=1):
         return pltpu.make_async_remote_copy(
             src_ref=own.at[pl.ds(lo, size)], dst_ref=land_l.at[pl.ds(lo, size)],
             send_sem=send_r.at[c], recv_sem=recv_l.at[c],
             device_id=(leaf + 1, samp), device_id_type=MESH,
         )
 
-    def to_left(c):
-        lo, size = (0, half) if c == 0 else (half + chunk * (c - 1), chunk)
+    def to_left(c, lo, size=1):
         return pltpu.make_async_remote_copy(
             src_ref=own.at[pl.ds(lo, size)], dst_ref=land_r.at[pl.ds(lo, size)],
             send_sem=send_l.at[c], recv_sem=recv_r.at[c],
             device_id=(leaf - 1, samp), device_id_type=MESH,
         )
 
-    for c in range(steps + 1):
+    @pl.when(leaf < n_leaf - 1)
+    def _():
+        to_right(0, half, half).start()
+
+    @pl.when(leaf > 0)
+    def _():
+        to_left(0, 0, half).start()
+
+    def send_pair(j, carry):
         @pl.when(leaf < n_leaf - 1)
         def _():
-            to_right(c).start()
+            to_right(j + 1, half - 1 - j).start()
 
         @pl.when(leaf > 0)
         def _():
-            to_left(c).start()
+            to_left(j + 1, half + j).start()
+
+        return carry
+
+    lax.fori_loop(0, steps, send_pair, 0)
 
     for r in range(rank * rank // 128):
         for src, dst in ((inner_ref, inner_v), (upper_ref, upper_v)):
@@ -135,7 +144,9 @@
         mat = upper_v[pl.ds(pl.multiple_of(node * rank, rank), rank), :][:, :rank].astype(BF16)
         rows = eye if rows is None else jnp.concatenate([eye, rows], axis=0)
         rows = chain_step(rows, mat)
-    paths[nodes] = rows
+    rows_high, rows_low = split(rows)
+    ascend[...] = jnp.concatenate([rows_high, rows_high, rows_low], axis=1)
+    paths[nodes] = eye
 
     def children(q):
         mats = inner_v[pl.ds(pl.multiple_of(q * 2 * rank, 2 * rank), 2 * rank), :]
@@ -152,11 +163,10 @@
 
     def leaf_pair(q, carry):
         high, low = split(children(q))
-        leaf_high[q] = high
-        leaf_low[q] = low
-        return carry
-
-    lax.fori_loop(0, pairs, leaf_pair, 0)
+        leaf_path[q] = jnp.concatenate([high, high, low], axis=1)
+        return carry
+
+    lax.fori_loop(0, pairs, leaf_pair, 0, unroll=4)
 
     load_samples.wait()
 
@@ -164,7 +174,7 @@
         packed[u] = pair_tile(samples_v, u)
         return carry
 
-    lax.fori_loop(0, pairs, pack_samples, 0)
+    lax.fori_loop(0, pairs, pack_samples, 0, unroll=4)
     up_acc[...] = jnp.zeros_like(up_acc)
     load_basis.wait()
     load_near.wait()
@@ -177,9 +187,9 @@
         tiles = []
         for k in range(slots):
             at = jnp.clip(index_ref[k, p] - base, 0, 3 * leaf_count - 1)
-            want = jnp.where(k < count_ref[p], at % 2, 2)
+            want = jnp.where(k < count_ref[p], at & 1, 2)
             mask = (lane_half == want).astype(F32).astype(BF16)
-            tiles.append(held[at // 2] * mask)
+            tiles.append(held[lax.shift_right_logical(at, 1)] * mask)
         left = jnp.concatenate([near_v[p, k] for k in range(slots)], axis=1)
         total = dot(left, jnp.concatenate(tiles, axis=0))
         return total + pltpu.roll(total, 64, 1)
@@ -209,11 +219,7 @@
             gram_send[t, pl.ds(pl.multiple_of(w * part, part), part), :] = (
                 gram[t * part:(t + 1) * part].astype(gram_send.dtype)
             )
-        path_high, path_low = leaf_high[u], leaf_low[u]
-        up_acc[...] += dot(
-            jnp.concatenate([path_high, path_high, path_low], axis=1),
-            jnp.concatenate([block_high, block_low, block_high], axis=0),
-        )
+        return dot(leaf_path[u], jnp.concatenate([block_high, block_low, block_high], axis=0))
 
     def accept(land, at_held, lo, size):
         def body(i, carry):
@@ -224,15 +230,15 @@
 
     @pl.when(leaf > 0)
     def _():
-        to_right(0).wait_recv()
+        to_right(0, half, half).wait_recv()
         accept(land_l, 0, half, half)
 
     @pl.when(leaf < n_leaf - 1)
     def _():
-        to_left(0).wait_recv()
+        to_left(0, 0, half).wait_recv()
         accept(land_r, 2 * pairs, 0, half)
 
-    span = 2 * chunk * part
+    span = 2 * part
 
     def gram_copy(d, j):
         at = pl.ds(pl.multiple_of(j * span, span), span)
@@ -243,37 +249,35 @@
         )
 
     def out_copy(j, side):
-        lo = 2 * (half - chunk * (j + 1)) if side == 0 else 2 * (half + chunk * j)
-        at = pl.ds(lo, 2 * chunk)
+        at = pl.ds(2 * (half - 1 - j) if side == 0 else 2 * (half + j), 2)
         return pltpu.make_async_copy(coeff_v.at[at], coeff_hbm.at[at], out_sem.at[side, j])
 
-    for j in range(steps):
-        lo_l = half - chunk * (j + 1)
-        lo_r = half + chunk * j
+    def step(j, carry):
+        lo_l = half - 1 - j
+        lo_r = half + j
 
         @pl.when(leaf > 0)
         def _():
-            to_right(j + 1).wait_recv()
-            accept(land_l, 0, lo_l, chunk)
+            to_right(j + 1, lo_l).wait_recv()
+            held[lo_l] = land_l[lo_l]
 
         @pl.when(leaf < n_leaf - 1)
         def _():
-            to_left(j + 1).wait_recv()
-            accept(land_r, 2 * pairs, lo_r, chunk)
-
-        def body(i, carry):
-            process(lo_l + i, 2 * chunk * j + i)
-            process(lo_r + i, 2 * chunk * j + chunk + i)
-            return carry
-
-        lax.fori_loop(0, chunk, body, 0)
+            to_left(j + 1, lo_r).wait_recv()
+            held[2 * pairs + lo_r] = land_r[lo_r]
+
+        up_acc[...] += process(lo_l, 2 * j) + process(lo_r, 2 * j + 1)
         for d in range(1, n_samp):
             gram_copy(d, j).start()
         out_copy(j, 0).start()
         out_copy(j, 1).start()
+        return carry
+
+    lax.fori_loop(0, steps, step, 0)
 
     total = up_acc[...]
-    total = total + pltpu.roll(total, 64, 1)
+    total_high, total_low = split(total + pltpu.roll(total, 64, 1))
+    total = dot(ascend[...], jnp.concatenate([total_high, total_low, total_high], axis=0))
     side = rank // 2
     for h in range(heights):
         up_send[h * side:(h + 1) * side] = jnp.where(
@@ -292,12 +296,14 @@
     for d in range(1, n_leaf):
         up_copy(d).start()
 
-    for j in range(steps):
+    def gram_wait(j, carry):
         for d in range(1, n_samp):
             gram_copy(d, j).wait_recv()
+        return carry
+
+    lax.fori_loop(0, steps, gram_wait, 0)
     for w in range(pairs):
-        j, i = divmod(w, 2 * chunk)
-        u = half - chunk * (j + 1) + i if i < chunk else half + chunk * j + i - chunk
+        u = half - 1 - w // 2 if w % 2 == 0 else half + w // 2
         at = slice(w * part, (w + 1) * part)
         value = gram_send[samp, at, :].astype(F32)
         for d in range(1, n_samp):
@@ -325,22 +331,44 @@
         ancestor_ref[h, 0:side, :] = value[:, :width]
         ancestor_ref[h, side:rank, :] = pltpu.roll(value, 64, 1)[:, :width]
 
-    for c in range(steps + 1):
+    @pl.when(leaf < n_leaf - 1)
+    def _():
+        to_right(0, half, half).wait_send()
+
+    @pl.when(leaf > 0)
+    def _():
+        to_left(0, 0, half).wait_send()
+
+    def finish(j, carry):
         @pl.when(leaf < n_leaf - 1)
         def _():
-            to_right(c).wait_send()
+            to_right(j + 1, half - 1 - j).wait_send()
 
         @pl.when(leaf > 0)
         def _():
-            to_left(c).wait_send()
-
-    for j in range(steps):
+            to_left(j + 1, half + j).wait_send()
+
         for d in range(1, n_samp):
             gram_copy(d, j).wait_send()
         out_copy(j, 0).wait()
         out_copy(j, 1).wait()
+        return carry
+
+    lax.fori_loop(0, steps, finish, 0)
     for d in range(1, n_leaf):
         up_copy(d).wait_send()
+
+
+def deliver(count, *refs):
+    sources, targets, sems = refs[:count], refs[count:-1], refs[-1]
+    copies = [
+        pltpu.make_async_copy(source, target, sems.at[i])
+        for i, (source, target) in enumerate(zip(sources, targets))
+    ]
+    for copy in copies:
+        copy.start()
+    for copy in copies:
+        copy.wait()
 
 
 def shards(
@@ -350,7 +378,7 @@
     leaf_count, rank, leaf_size = leaf_basis.shape
     width = samples.shape[1]
     pairs = leaf_count // 2
-    steps = pairs // 4
+    steps = pairs // 2
     heights = n_leaf.bit_length() - 1
     part = rank // n_samp
     nodes = inner_transfer.shape[0]
@@ -382,10 +410,10 @@
             pltpu.VMEM((pairs, leaf_size, 128), BF16),
             pltpu.VMEM((nodes * rank, 128), F32),
             pltpu.VMEM((upper_nodes * rank, 128), F32),
-            pltpu.VMEM((nodes + 1, heights * rank, rank), F32),
-            pltpu.VMEM((pairs, heights * rank, 128), BF16),
-            pltpu.VMEM((pairs, heights * rank, 128), BF16),
-            pltpu.VMEM((heights * rank, 128), F32),
+            pltpu.VMEM((nodes + 1, rank, rank), F32),
+            pltpu.VMEM((heights * rank, 3 * rank), BF16),
+            pltpu.VMEM((pairs, rank, 384), BF16),
+            pltpu.VMEM((rank, 128), F32),
             pltpu.VMEM((heights * rank // 2, 128), F32),
             pltpu.VMEM((n_leaf - 1, heights * rank // 2, 128), F32),
             pltpu.VMEM((n_samp, pairs * part, 128), wire),
@@ -403,7 +431,15 @@
             collective_id=0, has_side_effects=True, vmem_limit_bytes=56 * 1024 * 1024
         ),
     )(near_index, near_count, inner_transfer, upper_transfer, omega, samples, leaf_basis, near_blocks)
-    return coeffs, gram, ancestors[None]
+    results = (coeffs, gram, ancestors[None])
+    return pl.pallas_call(
+        functools.partial(deliver, len(results)),
+        out_shape=tuple(jax.ShapeDtypeStruct(x.shape, x.dtype) for x in results),
+        in_specs=[hbm] * len(results),
+        out_specs=(hbm,) * len(results),
+        scratch_shapes=[dma((len(results),))],
+        compiler_params=pltpu.CompilerParams(vmem_limit_bytes=62 * 1024 * 1024),
+    )(*results)
 
 
 def solution(mesh):

time: 50.9 us -> 84 us (1.65)
  Pallas kernels: 44.6 us -> 83.1 us
  local copies, waits for them, and re-layouts: 5.41 us -> 0 us
    pallas_call x0 -> x1, Pallas kernels: none -> 39.8 us  [shards(): pl.pallas_call(functools.partial(deliver, len(results)), out_shape=tuple(...]
    unnamed x3 -> x0, local copies, waits for them, and re-layouts: 5.41 us -> none
    pallas_call x1, Pallas kernels: 44.6 us -> 43.3 us  [shards(): pl.pallas_call(functools.partial(kernel, n_leaf, n_samp, width * n_samp),...]
where the time goes in v2:
time: 84 us; the launch traced here: 83.8 us
  Pallas kernels  83.1 us (99%)
    pallas_call x1, Pallas kernels, shards(): pl.pallas_call(functools.partial(kernel, n_leaf, n_samp, width * n_samp),...  43.3 us
    pallas_call x1, Pallas kernels, shards(): pl.pallas_call(functools.partial(deliver, len(results)), out_shape=tuple(...  39.8 us

profile of v2, /device:TPU:0, one launch (start us, length us, event | category | flops | bytes accessed | tf_op | source)
XLA Modules:
  0.0 83.8 jit_solution(13750596114886658903)
XLA Ops:
  0.6 43.3 %shard_map.103 = (f32[32,64,64]{2,1,0:T(8,128)}, f32[32,1024]{1,0:T(8,128)}, f32[3,64,64]{2,1,0:T(8,128)}) custom-call(s32[8,32]{1,0:T(8,128)} %bitcast.7, s32[32]{0:T(128)} %count_ref.1, bf16[62,4096]{1,0:T(8,128)(2,1)} %inner_ref.1, bf16[14,4096]{1,0:T(8,128)(2,1)} %upper_ref.1, bf16[64,4096]{1,0:T(8,128)(2,1)} %bitcast.4, bf16[64,4096]{1,0:T(8,128)(2,1)} %bitcast.5, ...), custom_call_target="tpu_custom_call" | custom-call | tf_op jit(solution)/shard_map/pallas_call | solution.py:392
  43.9 39.8 %shard_map.104 = (f32[32,64,64]{2,1,0:T(8,128)}, f32[32,1024]{1,0:T(8,128)}, f32[1,3,64,64]{3,2,1,0:T(8,128)}) custom-call(f32[32,64,64]{2,1,0:T(8,128)} %get-tuple-element.6.refs_0_, f32[32,1024]{1,0:T(8,128)} %get-tuple-element.7.refs_1_, f32[1,3,64,64]{3,2,1,0:T(8,128)} %bitcast.6), custom_call_target="tpu_custom_call" | custom-call | tf_op jit(solution)/shard_map/pallas_call | solution.py:435

commit v3 on v2

--- a/solution.py
+++ b/solution.py
@@ -36,7 +36,7 @@
     n_leaf, n_samp, total_columns,
     index_ref, count_ref, inner_ref, upper_ref, omega_hbm, samples_hbm, basis_hbm, near_hbm,
     coeff_hbm, gram_ref, ancestor_ref,
-    omega_v, samples_v, basis_v, near_v, own, land_l, land_r, held, packed,
+    omega_v, samples_v, basis_v, near_v, land_l, land_r, held,
     inner_v, upper_v, paths, ascend, leaf_path, up_acc, up_send, up_recv,
     gram_send, gram_recv, gram_sum, gram_mix, coeff_v,
     load_sem, near_sem, send_l, send_r, recv_l, recv_r,
@@ -69,34 +69,22 @@
     for d in range(1, n_samp):
         pl.semaphore_signal(barrier, inc=1, device_id=(leaf, samp ^ d), device_id_type=MESH)
 
-    load_omega.wait()
-
-    def pair_tile(src, u):
-        at = pl.multiple_of(u * 2 * leaf_size, 2 * leaf_size)
-        rows = jnp.concatenate(
-            [src[:, pl.ds(at, leaf_size)], src[:, pl.ds(at + leaf_size, leaf_size)]], axis=0
-        )
-        return rows.T
-
-    def pack_omega(u, carry):
-        tile = pair_tile(omega_v, u)
-        own[u] = tile
-        held[pairs + u] = tile
-        return carry
-
-    lax.fori_loop(0, pairs, pack_omega, 0, unroll=4)
     pl.semaphore_wait(barrier, n_leaf + n_samp - 2)
+
+    def lanes(lo, size=1):
+        unit = 2 * leaf_size
+        return pl.ds(pl.multiple_of(lo * unit, unit), size * unit)
 
     def to_right(c, lo, size=1):
         return pltpu.make_async_remote_copy(
-            src_ref=own.at[pl.ds(lo, size)], dst_ref=land_l.at[pl.ds(lo, size)],
+            src_ref=omega_hbm.at[:, lanes(lo, size)], dst_ref=land_l.at[:, lanes(lo, size)],
             send_sem=send_r.at[c], recv_sem=recv_l.at[c],
             device_id=(leaf + 1, samp), device_id_type=MESH,
         )
 
     def to_left(c, lo, size=1):
         return pltpu.make_async_remote_copy(
-            src_ref=own.at[pl.ds(lo, size)], dst_ref=land_r.at[pl.ds(lo, size)],
+            src_ref=omega_hbm.at[:, lanes(lo, size)], dst_ref=land_r.at[:, lanes(lo, size)],
             send_sem=send_l.at[c], recv_sem=recv_r.at[c],
             device_id=(leaf - 1, samp), device_id_type=MESH,
         )
@@ -168,18 +156,25 @@
 
     lax.fori_loop(0, pairs, leaf_pair, 0, unroll=4)
 
+    def accept(src, at_held, lo):
+        both = src[:, lanes(lo)]
+        held[at_held + 2 * lo] = both[:, :leaf_size]
+        held[at_held + 2 * lo + 1] = both[:, leaf_size:]
+
+    def accept_many(src, at_held, lo, size):
+        def body(i, carry):
+            accept(src, at_held, lo + i)
+            return carry
+
+        lax.fori_loop(0, size, body, 0, unroll=4)
+
+    load_omega.wait()
+    accept_many(omega_v, leaf_count, 0, pairs)
+    up_acc[...] = jnp.zeros_like(up_acc)
     load_samples.wait()
-
-    def pack_samples(u, carry):
-        packed[u] = pair_tile(samples_v, u)
-        return carry
-
-    lax.fori_loop(0, pairs, pack_samples, 0, unroll=4)
-    up_acc[...] = jnp.zeros_like(up_acc)
     load_basis.wait()
     load_near.wait()
 
-    lane_half = lax.broadcasted_iota(jnp.int32, (1, 128), 1) // 64
     lower = lax.broadcasted_iota(jnp.int32, (leaf_size, 128), 1) < 64
     base = leaf * leaf_count - leaf_count
 
@@ -187,18 +182,18 @@
         tiles = []
         for k in range(slots):
             at = jnp.clip(index_ref[k, p] - base, 0, 3 * leaf_count - 1)
-            want = jnp.where(k < count_ref[p], at & 1, 2)
-            mask = (lane_half == want).astype(F32).astype(BF16)
-            tiles.append(held[lax.shift_right_logical(at, 1)] * mask)
-        left = jnp.concatenate([near_v[p, k] for k in range(slots)], axis=1)
-        total = dot(left, jnp.concatenate(tiles, axis=0))
-        return total + pltpu.roll(total, 64, 1)
+            live = jnp.where(k < count_ref[p], 1.0, 0.0)
+            tiles.append(held[at] * jnp.full((1, leaf_size), live, F32).astype(BF16))
+        blocks = jnp.concatenate([near_v[p, k] for k in range(slots)], axis=1)
+        return dot_nt(jnp.concatenate(tiles, axis=1), blocks)
 
     def process(u, w):
-        near = jnp.where(lower, near_product(2 * u), near_product(2 * u + 1))
-        far = (packed[u].astype(F32) - near).astype(BF16)
+        near = jnp.concatenate([near_product(2 * u), near_product(2 * u + 1)], axis=0)
+        mine = samples_v[:, lanes(u)]
+        mine = jnp.concatenate([mine[:, :leaf_size], mine[:, leaf_size:]], axis=0)
+        far = (mine.astype(F32) - near).astype(BF16)
         basis = basis_v[pl.ds(2 * u, 2)].reshape(2 * rank, leaf_size)
-        both = dot(basis, far)
+        both = dot_nt(basis, far)
         top, bottom = both[:rank], both[rank:]
         coeff_v[2 * u] = top[:, :width]
         coeff_v[2 * u + 1] = pltpu.roll(bottom, 64, 1)[:, :width]
@@ -221,22 +216,15 @@
             )
         return dot(leaf_path[u], jnp.concatenate([block_high, block_low, block_high], axis=0))
 
-    def accept(land, at_held, lo, size):
-        def body(i, carry):
-            held[at_held + lo + i] = land[lo + i]
-            return carry
-
-        lax.fori_loop(0, size, body, 0)
-
     @pl.when(leaf > 0)
     def _():
         to_right(0, half, half).wait_recv()
-        accept(land_l, 0, half, half)
+        accept_many(land_l, 0, half, half)
 
     @pl.when(leaf < n_leaf - 1)
     def _():
         to_left(0, 0, half).wait_recv()
-        accept(land_r, 2 * pairs, 0, half)
+        accept_many(land_r, 2 * leaf_count, 0, half)
 
     span = 2 * part
 
@@ -259,12 +247,12 @@
         @pl.when(leaf > 0)
         def _():
             to_right(j + 1, lo_l).wait_recv()
-            held[lo_l] = land_l[lo_l]
+            accept(land_l, 0, lo_l)
 
         @pl.when(leaf < n_leaf - 1)
         def _():
             to_left(j + 1, lo_r).wait_recv()
-            held[2 * pairs + lo_r] = land_r[lo_r]
+            accept(land_r, 2 * leaf_count, lo_r)
 
         up_acc[...] += process(lo_l, 2 * j) + process(lo_r, 2 * j + 1)
         for d in range(1, n_samp):
@@ -360,15 +348,17 @@
 
 
 def deliver(count, *refs):
-    sources, targets, sems = refs[:count], refs[count:-1], refs[-1]
-    copies = [
-        pltpu.make_async_copy(source, target, sems.at[i])
-        for i, (source, target) in enumerate(zip(sources, targets))
-    ]
-    for copy in copies:
-        copy.start()
-    for copy in copies:
-        copy.wait()
+    sources, targets, rooms = refs[:count], refs[count:2 * count], refs[2 * count:3 * count]
+    sems = refs[-1]
+    reads = [pltpu.make_async_copy(sources[i], rooms[i], sems.at[0, i]) for i in range(count)]
+    writes = [pltpu.make_async_copy(rooms[i], targets[i], sems.at[1, i]) for i in range(count)]
+    for read in reads:
+        read.start()
+    for read, write in zip(reads, writes):
+        read.wait()
+        write.start()
+    for write in writes:
+        write.wait()
 
 
 def shards(
@@ -403,11 +393,9 @@
             pltpu.VMEM(samples.shape, BF16),
             pltpu.VMEM(leaf_basis.shape, BF16),
             pltpu.VMEM(near_blocks.shape, BF16),
-            pltpu.VMEM((pairs, leaf_size, 128), BF16),
-            pltpu.VMEM((pairs, leaf_size, 128), BF16),
-            pltpu.VMEM((pairs, leaf_size, 128), BF16),
-            pltpu.VMEM((3 * pairs, leaf_size, 128), BF16),
-            pltpu.VMEM((pairs, leaf_size, 128), BF16),
+            pltpu.VMEM(omega.shape, BF16),
+            pltpu.VMEM(omega.shape, BF16),
+            pltpu.VMEM((3 * leaf_count, width, leaf_size), BF16),
             pltpu.VMEM((nodes * rank, 128), F32),
             pltpu.VMEM((upper_nodes * rank, 128), F32),
             pltpu.VMEM((nodes + 1, rank, rank), F32),
@@ -437,7 +425,7 @@
         out_shape=tuple(jax.ShapeDtypeStruct(x.shape, x.dtype) for x in results),
         in_specs=[hbm] * len(results),
         out_specs=(hbm,) * len(results),
-        scratch_shapes=[dma((len(results),))],
+        scratch_shapes=[pltpu.VMEM(x.shape, x.dtype) for x in results] + [dma((2, len(results)))],
         compiler_params=pltpu.CompilerParams(vmem_limit_bytes=62 * 1024 * 1024),
     )(*results)
 

time: 84 us -> 45.9 us (0.55)
  Pallas kernels: 83.1 us -> 45.1 us
    pallas_call x1, Pallas kernels: 39.8 us -> 2.31 us  [shards(): pl.pallas_call(functools.partial(deliver, len(results)), out_shape=tuple(...]
where the time goes in v3:
time: 45.9 us; the launch traced here: 45.7 us
  Pallas kernels  45.1 us (98%)
  between operations  0.64 us (1%)
    pallas_call x1, Pallas kernels, shards(): pl.pallas_call(functools.partial(kernel, n_leaf, n_samp, width * n_samp),...  42.7 us
    pallas_call x1, Pallas kernels, shards(): pl.pallas_call(functools.partial(deliver, len(results)), out_shape=tuple(...  2.31 us

profile of v3, /device:TPU:0, one launch (start us, length us, event | category | flops | bytes accessed | tf_op | source)
XLA Modules:
  0.0 45.7 jit_solution(13743315751966230851)
XLA Ops:
  0.6 42.7 %shard_map.103 = (f32[32,64,64]{2,1,0:T(8,128)}, f32[32,1024]{1,0:T(8,128)}, f32[3,64,64]{2,1,0:T(8,128)}) custom-call(s32[8,32]{1,0:T(8,128)} %bitcast.7, s32[32]{0:T(128)} %count_ref.1, bf16[62,4096]{1,0:T(8,128)(2,1)} %inner_ref.1, bf16[14,4096]{1,0:T(8,128)(2,1)} %upper_ref.1, bf16[64,4096]{1,0:T(8,128)(2,1)} %bitcast.4, bf16[64,4096]{1,0:T(8,128)(2,1)} %bitcast.5, ...), custom_call_target="tpu_custom_call" | custom-call | tf_op jit(solution)/shard_map/pallas_call | solution.py:382
  43.4 2.3 %shard_map.104 = (f32[32,64,64]{2,1,0:T(8,128)}, f32[32,1024]{1,0:T(8,128)}, f32[1,3,64,64]{3,2,1,0:T(8,128)}) custom-call(f32[32,64,64]{2,1,0:T(8,128)} %get-tuple-element.6.refs_0_, f32[32,1024]{1,0:T(8,128)} %get-tuple-element.7.refs_1_, f32[1,3,64,64]{3,2,1,0:T(8,128)} %bitcast.6), custom_call_target="tpu_custom_call" | custom-call | tf_op jit(solution)/shard_map/pallas_call | solution.py:423

commit v4 on v3

--- a/solution.py
+++ b/solution.py
@@ -71,51 +71,64 @@
 
     pl.semaphore_wait(barrier, n_leaf + n_samp - 2)
 
-    def lanes(lo, size=1):
+    def lanes(pair):
         unit = 2 * leaf_size
-        return pl.ds(pl.multiple_of(lo * unit, unit), size * unit)
-
-    def to_right(c, lo, size=1):
+        return pl.ds(pl.multiple_of(pair * unit, unit), unit)
+
+    def to_right(c):
+        at = lanes(pairs - 1 - c)
         return pltpu.make_async_remote_copy(
-            src_ref=omega_hbm.at[:, lanes(lo, size)], dst_ref=land_l.at[:, lanes(lo, size)],
+            src_ref=omega_hbm.at[:, at], dst_ref=land_l.at[:, at],
             send_sem=send_r.at[c], recv_sem=recv_l.at[c],
             device_id=(leaf + 1, samp), device_id_type=MESH,
         )
 
-    def to_left(c, lo, size=1):
+    def to_left(c):
+        at = lanes(c)
         return pltpu.make_async_remote_copy(
-            src_ref=omega_hbm.at[:, lanes(lo, size)], dst_ref=land_r.at[:, lanes(lo, size)],
+            src_ref=omega_hbm.at[:, at], dst_ref=land_r.at[:, at],
             send_sem=send_l.at[c], recv_sem=recv_r.at[c],
             device_id=(leaf - 1, samp), device_id_type=MESH,
         )
 
-    @pl.when(leaf < n_leaf - 1)
-    def _():
-        to_right(0, half, half).start()
-
-    @pl.when(leaf > 0)
-    def _():
-        to_left(0, 0, half).start()
-
-    def send_pair(j, carry):
+    def send(c):
         @pl.when(leaf < n_leaf - 1)
         def _():
-            to_right(j + 1, half - 1 - j).start()
+            to_right(c).start()
 
         @pl.when(leaf > 0)
         def _():
-            to_left(j + 1, half + j).start()
-
-        return carry
-
-    lax.fori_loop(0, steps, send_pair, 0)
-
-    for r in range(rank * rank // 128):
+            to_left(c).start()
+
+    window = 4
+
+    def pump(c):
+        @pl.when(leaf < n_leaf - 1)
+        def _():
+            to_right(c).wait_send()
+
+        @pl.when(leaf > 0)
+        def _():
+            to_left(c).wait_send()
+
+        @pl.when(c + window < pairs)
+        def _():
+            send(c + window)
+
+    for c in range(window):
+        send(c)
+
+    lines = rank * rank // 128
+    for r in range(lines):
+        if r % (lines // 2) == 0 and r > 0:
+            pump(r // (lines // 2) - 1)
         for src, dst in ((inner_ref, inner_v), (upper_ref, upper_v)):
             count = src.shape[0]
             tile = src[:, 128 * r:128 * r + 128].astype(F32)
             dst[pl.ds(2 * r, count, stride=rank), :] = tile
             dst[pl.ds(2 * r + 1, count, stride=rank), :] = pltpu.roll(tile, 64, 1)
+
+    pump(1)
 
     eye = (
         lax.broadcasted_iota(jnp.int32, (rank, rank), 0)
@@ -145,31 +158,34 @@
         both = children(q)
         paths[2 * q] = both[:, :rank]
         paths[2 * q + 1] = pltpu.roll(both, 64, 1)[:, :rank]
+
+        @pl.when(i % 3 == 2)
+        def _():
+            pump(2 + i // 3)
+
         return carry
 
     lax.fori_loop(0, pairs - 1, inner_pair, 0)
 
-    def leaf_pair(q, carry):
-        high, low = split(children(q))
-        leaf_path[q] = jnp.concatenate([high, high, low], axis=1)
-        return carry
-
-    lax.fori_loop(0, pairs, leaf_pair, 0, unroll=4)
+    pumped = 2 + (pairs - 1) // 3
+
+    def leaf_pairs(g, carry):
+        for i in range(half):
+            high, low = split(children(g * half + i))
+            leaf_path[g * half + i] = jnp.concatenate([high, high, low], axis=1)
+        pump(pumped + g)
+        return carry
+
+    lax.fori_loop(0, 2, leaf_pairs, 0)
 
     def accept(src, at_held, lo):
         both = src[:, lanes(lo)]
         held[at_held + 2 * lo] = both[:, :leaf_size]
         held[at_held + 2 * lo + 1] = both[:, leaf_size:]
 
-    def accept_many(src, at_held, lo, size):
-        def body(i, carry):
-            accept(src, at_held, lo + i)
-            return carry
-
-        lax.fori_loop(0, size, body, 0, unroll=4)
-
     load_omega.wait()
-    accept_many(omega_v, leaf_count, 0, pairs)
+    for i in range(pairs):
+        accept(omega_v, leaf_count, i)
     up_acc[...] = jnp.zeros_like(up_acc)
     load_samples.wait()
     load_basis.wait()
@@ -216,15 +232,22 @@
             )
         return dot(leaf_path[u], jnp.concatenate([block_high, block_low, block_high], axis=0))
 
-    @pl.when(leaf > 0)
-    def _():
-        to_right(0, half, half).wait_recv()
-        accept_many(land_l, 0, half, half)
-
-    @pl.when(leaf < n_leaf - 1)
-    def _():
-        to_left(0, 0, half).wait_recv()
-        accept_many(land_r, 2 * leaf_count, 0, half)
+    def receive(c):
+        @pl.when(leaf > 0)
+        def _():
+            to_right(c).wait_recv()
+            accept(land_l, 0, pairs - 1 - c)
+
+        @pl.when(leaf < n_leaf - 1)
+        def _():
+            to_left(c).wait_recv()
+            accept(land_r, 2 * leaf_count, c)
+
+    def first(c, carry):
+        receive(c)
+        return carry
+
+    lax.fori_loop(0, half, first, 0)
 
     span = 2 * part
 
@@ -244,21 +267,17 @@
         lo_l = half - 1 - j
         lo_r = half + j
 
-        @pl.when(leaf > 0)
-        def _():
-            to_right(j + 1, lo_l).wait_recv()
-            accept(land_l, 0, lo_l)
-
-        @pl.when(leaf < n_leaf - 1)
-        def _():
-            to_left(j + 1, lo_r).wait_recv()
-            accept(land_r, 2 * leaf_count, lo_r)
-
+        receive(half + j)
         up_acc[...] += process(lo_l, 2 * j) + process(lo_r, 2 * j + 1)
         for d in range(1, n_samp):
             gram_copy(d, j).start()
         out_copy(j, 0).start()
         out_copy(j, 1).start()
+
+        @pl.when(j < steps - 1)
+        def _():
+            pump(half + 1 + j)
+
         return carry
 
     lax.fori_loop(0, steps, step, 0)
@@ -319,23 +338,7 @@
         ancestor_ref[h, 0:side, :] = value[:, :width]
         ancestor_ref[h, side:rank, :] = pltpu.roll(value, 64, 1)[:, :width]
 
-    @pl.when(leaf < n_leaf - 1)
-    def _():
-        to_right(0, half, half).wait_send()
-
-    @pl.when(leaf > 0)
-    def _():
-        to_left(0, 0, half).wait_send()
-
     def finish(j, carry):
-        @pl.when(leaf < n_leaf - 1)
-        def _():
-            to_right(j + 1, half - 1 - j).wait_send()
-
-        @pl.when(leaf > 0)
-        def _():
-            to_left(j + 1, half + j).wait_send()
-
         for d in range(1, n_samp):
             gram_copy(d, j).wait_send()
         out_copy(j, 0).wait()
@@ -410,7 +413,7 @@
             pltpu.VMEM((part // 2 * leaf_count, 128), F32),
             pltpu.VMEM((leaf_count, rank, width), F32),
             dma((3,)), dma,
-            dma((steps + 1,)), dma((steps + 1,)), dma((steps + 1,)), dma((steps + 1,)),
+            dma((pairs,)), dma((pairs,)), dma((pairs,)), dma((pairs,)),
             dma((n_samp - 1, steps)), dma((n_samp - 1, steps)),
             dma((n_leaf - 1,)), dma((n_leaf - 1,)),
             dma((2, steps)),

time: 45.9 us -> 44.2 us (0.963)
  Pallas kernels: 45.1 us -> 43.4 us
    pallas_call x1, Pallas kernels: 42.7 us -> 41.1 us  [shards(): pl.pallas_call(functools.partial(kernel, n_leaf, n_samp, width * n_samp),...]
where the time goes in v4:
time: 44.2 us; the launch traced here: 44.1 us
  Pallas kernels  43.4 us (98%)
  between operations  0.64 us (1%)
    pallas_call x1, Pallas kernels, shards(): pl.pallas_call(functools.partial(kernel, n_leaf, n_samp, width * n_samp),...  41.1 us
    pallas_call x1, Pallas kernels, shards(): pl.pallas_call(functools.partial(deliver, len(results)), out_shape=tuple(...  2.31 us

profile of v4, /device:TPU:0, one launch (start us, length us, event | category | flops | bytes accessed | tf_op | source)
XLA Modules:
  0.0 44.1 jit_solution(18370578496977555681)
XLA Ops:
  0.6 41.1 %shard_map.103 = (f32[32,64,64]{2,1,0:T(8,128)}, f32[32,1024]{1,0:T(8,128)}, f32[3,64,64]{2,1,0:T(8,128)}) custom-call(s32[8,32]{1,0:T(8,128)} %bitcast.7, s32[32]{0:T(128)} %count_ref.1, bf16[62,4096]{1,0:T(8,128)(2,1)} %inner_ref.1, bf16[14,4096]{1,0:T(8,128)(2,1)} %upper_ref.1, bf16[64,4096]{1,0:T(8,128)(2,1)} %bitcast.4, bf16[64,4096]{1,0:T(8,128)(2,1)} %bitcast.5, ...), custom_call_target="tpu_custom_call" | custom-call | tf_op jit(solution)/shard_map/pallas_call | solution.py:385
  41.7 2.3 %shard_map.104 = (f32[32,64,64]{2,1,0:T(8,128)}, f32[32,1024]{1,0:T(8,128)}, f32[1,3,64,64]{3,2,1,0:T(8,128)}) custom-call(f32[32,64,64]{2,1,0:T(8,128)} %get-tuple-element.6.refs_0_, f32[32,1024]{1,0:T(8,128)} %get-tuple-element.7.refs_1_, f32[1,3,64,64]{3,2,1,0:T(8,128)} %bitcast.6), custom_call_target="tpu_custom_call" | custom-call | tf_op jit(solution)/shard_map/pallas_call | solution.py:426

commit v5 on v4

--- a/solution.py
+++ b/solution.py
@@ -34,11 +34,11 @@
 
 def kernel(
     n_leaf, n_samp, total_columns,
-    index_ref, count_ref, inner_ref, upper_ref, omega_hbm, samples_hbm, basis_hbm, near_hbm,
+    index_ref, count_ref, inner_hbm, upper_hbm, omega_hbm, samples_hbm, basis_hbm, near_hbm,
     coeff_hbm, gram_ref, ancestor_ref,
-    omega_v, samples_v, basis_v, near_v, land_l, land_r, held,
+    inner_ref, upper_ref, omega_v, samples_v, basis_v, near_v, land_l, land_r, held,
     inner_v, upper_v, paths, ascend, leaf_path, up_acc, up_send, up_recv,
-    gram_send, gram_recv, gram_sum, gram_mix, coeff_v,
+    gram_send, gram_recv, gram_sum, gram_mix, coeff_v, far_v,
     load_sem, near_sem, send_l, send_r, recv_l, recv_r,
     gram_ssem, gram_rsem, up_ssem, up_rsem, out_sem,
 ):
@@ -58,6 +58,10 @@
     load_samples = pltpu.make_async_copy(samples_hbm, samples_v, load_sem.at[1])
     load_basis = pltpu.make_async_copy(basis_hbm, basis_v, load_sem.at[2])
     load_near = pltpu.make_async_copy(near_hbm, near_v, near_sem)
+    load_inner = pltpu.make_async_copy(inner_hbm, inner_ref, load_sem.at[3])
+    load_upper = pltpu.make_async_copy(upper_hbm, upper_ref, load_sem.at[4])
+    load_inner.start()
+    load_upper.start()
     load_omega.start()
     load_samples.start()
     load_basis.start()
@@ -118,6 +122,8 @@
     for c in range(window):
         send(c)
 
+    load_inner.wait()
+    load_upper.wait()
     lines = rank * rank // 128
     for r in range(lines):
         if r % (lines // 2) == 0 and r > 0:
@@ -203,11 +209,14 @@
         blocks = jnp.concatenate([near_v[p, k] for k in range(slots)], axis=1)
         return dot_nt(jnp.concatenate(tiles, axis=1), blocks)
 
-    def process(u, w):
+    def near_stage(u, w):
         near = jnp.concatenate([near_product(2 * u), near_product(2 * u + 1)], axis=0)
         mine = samples_v[:, lanes(u)]
         mine = jnp.concatenate([mine[:, :leaf_size], mine[:, leaf_size:]], axis=0)
-        far = (mine.astype(F32) - near).astype(BF16)
+        far_v[w] = (mine.astype(F32) - near).astype(BF16)
+
+    def post_stage(u, w):
+        far = far_v[w]
         basis = basis_v[pl.ds(2 * u, 2)].reshape(2 * rank, leaf_size)
         both = dot_nt(basis, far)
         top, bottom = both[:rank], both[rank:]
@@ -249,7 +258,7 @@
 
     lax.fori_loop(0, half, first, 0)
 
-    span = 2 * part
+    span = 4 * part
 
     def gram_copy(d, j):
         at = pl.ds(pl.multiple_of(j * span, span), span)
@@ -259,28 +268,47 @@
             device_id=(leaf, samp ^ d), device_id_type=MESH,
         )
 
-    def out_copy(j, side):
-        at = pl.ds(2 * (half - 1 - j) if side == 0 else 2 * (half + j), 2)
-        return pltpu.make_async_copy(coeff_v.at[at], coeff_hbm.at[at], out_sem.at[side, j])
+    quarter = leaf_count // 4
+
+    def out_copy(i):
+        at = pl.ds((quarter, 0, 3 * quarter)[i], (2 * quarter, quarter, quarter)[i])
+        return pltpu.make_async_copy(coeff_v.at[at], coeff_hbm.at[at], out_sem.at[i])
+
+    def nears(j):
+        near_stage(half - 1 - j, 2 * j)
+        near_stage(half + j, 2 * j + 1)
+
+    def posts(j):
+        up_acc[...] += post_stage(half - 1 - j, 2 * j) + post_stage(half + j, 2 * j + 1)
+
+    receive(half)
+    nears(0)
+    pump(half + 1)
 
     def step(j, carry):
-        lo_l = half - 1 - j
-        lo_r = half + j
-
         receive(half + j)
-        up_acc[...] += process(lo_l, 2 * j) + process(lo_r, 2 * j + 1)
-        for d in range(1, n_samp):
-            gram_copy(d, j).start()
-        out_copy(j, 0).start()
-        out_copy(j, 1).start()
+        posts(j - 1)
+        nears(j)
+
+        @pl.when(j % 2 == 0)
+        def _():
+            for d in range(1, n_samp):
+                gram_copy(d, j // 2 - 1).start()
 
         @pl.when(j < steps - 1)
         def _():
             pump(half + 1 + j)
 
-        return carry
-
-    lax.fori_loop(0, steps, step, 0)
+        @pl.when(j == steps // 2)
+        def _():
+            out_copy(0).start()
+
+        return carry
+
+    lax.fori_loop(1, steps, step, 0)
+    posts(steps - 1)
+    for d in range(1, n_samp):
+        gram_copy(d, steps // 2 - 1).start()
 
     total = up_acc[...]
     total_high, total_low = split(total + pltpu.roll(total, 64, 1))
@@ -302,13 +330,15 @@
 
     for d in range(1, n_leaf):
         up_copy(d).start()
+    out_copy(1).start()
+    out_copy(2).start()
 
     def gram_wait(j, carry):
         for d in range(1, n_samp):
             gram_copy(d, j).wait_recv()
         return carry
 
-    lax.fori_loop(0, steps, gram_wait, 0)
+    lax.fori_loop(0, steps // 2, gram_wait, 0)
     for w in range(pairs):
         u = half - 1 - w // 2 if w % 2 == 0 else half + w // 2
         at = slice(w * part, (w + 1) * part)
@@ -341,11 +371,11 @@
     def finish(j, carry):
         for d in range(1, n_samp):
             gram_copy(d, j).wait_send()
-        out_copy(j, 0).wait()
-        out_copy(j, 1).wait()
-        return carry
-
-    lax.fori_loop(0, steps, finish, 0)
+        return carry
+
+    lax.fori_loop(0, steps // 2, finish, 0)
+    for i in range(3):
+        out_copy(i).wait()
     for d in range(1, n_leaf):
         up_copy(d).wait_send()
 
@@ -389,9 +419,11 @@
             jax.ShapeDtypeStruct((leaf_count, part * rank), F32),
             jax.ShapeDtypeStruct((heights, rank, width), F32),
         ),
-        in_specs=[smem, smem, vmem, vmem, hbm, hbm, hbm, hbm],
+        in_specs=[smem, smem, hbm, hbm, hbm, hbm, hbm, hbm],
         out_specs=(hbm, vmem, vmem),
         scratch_shapes=[
+            pltpu.VMEM(inner_transfer.shape, BF16),
+            pltpu.VMEM(upper_transfer.shape, BF16),
             pltpu.VMEM(omega.shape, BF16),
             pltpu.VMEM(samples.shape, BF16),
             pltpu.VMEM(leaf_basis.shape, BF16),
@@ -412,11 +444,12 @@
             pltpu.VMEM((pairs * part, 128), F32),
             pltpu.VMEM((part // 2 * leaf_count, 128), F32),
             pltpu.VMEM((leaf_count, rank, width), F32),
-            dma((3,)), dma,
+            pltpu.VMEM((pairs, leaf_size, leaf_size), BF16),
+            dma((5,)), dma,
             dma((pairs,)), dma((pairs,)), dma((pairs,)), dma((pairs,)),
-            dma((n_samp - 1, steps)), dma((n_samp - 1, steps)),
+            dma((n_samp - 1, steps // 2)), dma((n_samp - 1, steps // 2)),
             dma((n_leaf - 1,)), dma((n_leaf - 1,)),
-            dma((2, steps)),
+            dma((3,)),
         ],
         compiler_params=pltpu.CompilerParams(
             collective_id=0, has_side_effects=True, vmem_limit_bytes=56 * 1024 * 1024

time: 44.2 us -> 42.7 us (0.966)
  Pallas kernels: 43.4 us -> 41.8 us
    pallas_call x1, Pallas kernels: 41.1 us -> 39.5 us  [shards(): pl.pallas_call(functools.partial(kernel, n_leaf, n_samp, width * n_samp),...]
where the time goes in v5:
time: 42.7 us; the launch traced here: 42.5 us
  Pallas kernels  41.8 us (98%)
  between operations  0.64 us (1%)
    pallas_call x1, Pallas kernels, shards(): pl.pallas_call(functools.partial(kernel, n_leaf, n_samp, width * n_samp),...  39.5 us
    pallas_call x1, Pallas kernels, shards(): pl.pallas_call(functools.partial(deliver, len(results)), out_shape=tuple(...  2.31 us

profile of v5, /device:TPU:0, one launch (start us, length us, event | category | flops | bytes accessed | tf_op | source)
XLA Modules:
  0.0 42.5 jit_solution(115952316907616591)
XLA Ops:
  0.6 39.5 %shard_map.103 = (f32[32,64,64]{2,1,0:T(8,128)}, f32[32,1024]{1,0:T(8,128)}, f32[3,64,64]{2,1,0:T(8,128)}) custom-call(s32[8,32]{1,0:T(8,128)} %bitcast.7, s32[32]{0:T(128)} %count_ref.1, bf16[62,4096]{1,0:T(8,128)(2,1)} %inner_hbm.1, bf16[14,4096]{1,0:T(8,128)(2,1)} %upper_hbm.1, bf16[64,4096]{1,0:T(8,128)(2,1)} %bitcast.4, bf16[64,4096]{1,0:T(8,128)(2,1)} %bitcast.5, ...), custom_call_target="tpu_custom_call" | custom-call | tf_op jit(solution)/shard_map/pallas_call | solution.py:415
  40.2 2.3 %shard_map.104 = (f32[32,64,64]{2,1,0:T(8,128)}, f32[32,1024]{1,0:T(8,128)}, f32[1,3,64,64]{3,2,1,0:T(8,128)}) custom-call(f32[32,64,64]{2,1,0:T(8,128)} %get-tuple-element.6.refs_0_, f32[32,1024]{1,0:T(8,128)} %get-tuple-element.7.refs_1_, f32[1,3,64,64]{3,2,1,0:T(8,128)} %bitcast.6), custom_call_target="tpu_custom_call" | custom-call | tf_op jit(solution)/shard_map/pallas_call | solution.py:459

commit v6 on v5

--- a/solution.py
+++ b/solution.py
@@ -104,37 +104,18 @@
         def _():
             to_left(c).start()
 
-    window = 4
-
-    def pump(c):
-        @pl.when(leaf < n_leaf - 1)
-        def _():
-            to_right(c).wait_send()
-
-        @pl.when(leaf > 0)
-        def _():
-            to_left(c).wait_send()
-
-        @pl.when(c + window < pairs)
-        def _():
-            send(c + window)
-
-    for c in range(window):
+    for c in range(half + 1):
         send(c)
 
     load_inner.wait()
     load_upper.wait()
     lines = rank * rank // 128
     for r in range(lines):
-        if r % (lines // 2) == 0 and r > 0:
-            pump(r // (lines // 2) - 1)
         for src, dst in ((inner_ref, inner_v), (upper_ref, upper_v)):
             count = src.shape[0]
             tile = src[:, 128 * r:128 * r + 128].astype(F32)
             dst[pl.ds(2 * r, count, stride=rank), :] = tile
             dst[pl.ds(2 * r + 1, count, stride=rank), :] = pltpu.roll(tile, 64, 1)
-
-    pump(1)
 
     eye = (
         lax.broadcasted_iota(jnp.int32, (rank, rank), 0)
@@ -155,34 +136,15 @@
     ascend[...] = jnp.concatenate([rows_high, rows_high, rows_low], axis=1)
     paths[nodes] = eye
 
-    def children(q):
-        mats = inner_v[pl.ds(pl.multiple_of(q * 2 * rank, 2 * rank), 2 * rank), :]
-        return chain_step(paths[leaf_count + q], mats[:, :rank].astype(BF16))
-
-    def inner_pair(i, carry):
-        q = leaf_count - 2 - i
-        both = children(q)
-        paths[2 * q] = both[:, :rank]
-        paths[2 * q + 1] = pltpu.roll(both, 64, 1)[:, :rank]
-
-        @pl.when(i % 3 == 2)
-        def _():
-            pump(2 + i // 3)
-
-        return carry
-
-    lax.fori_loop(0, pairs - 1, inner_pair, 0)
-
-    pumped = 2 + (pairs - 1) // 3
-
-    def leaf_pairs(g, carry):
-        for i in range(half):
-            high, low = split(children(g * half + i))
-            leaf_path[g * half + i] = jnp.concatenate([high, high, low], axis=1)
-        pump(pumped + g)
-        return carry
-
-    lax.fori_loop(0, 2, leaf_pairs, 0)
+    for q in reversed(range(leaf_count - 1)):
+        mats = inner_v[q * 2 * rank:(q + 1) * 2 * rank, :]
+        both = chain_step(paths[leaf_count + q], mats[:, :rank].astype(BF16))
+        if q < pairs:
+            high, low = split(both)
+            leaf_path[q] = jnp.concatenate([high, high, low], axis=1)
+        else:
+            paths[2 * q] = both[:, :rank]
+            paths[2 * q + 1] = pltpu.roll(both, 64, 1)[:, :rank]
 
     def accept(src, at_held, lo):
         both = src[:, lanes(lo)]
@@ -252,11 +214,12 @@
             to_left(c).wait_recv()
             accept(land_r, 2 * leaf_count, c)
 
-    def first(c, carry):
+    send(half + 1)
+    for c in range(half):
         receive(c)
-        return carry
-
-    lax.fori_loop(0, half, first, 0)
+        if c == half // 2:
+            send(half + 2)
+    send(half + 3)
 
     span = 4 * part
 
@@ -282,11 +245,16 @@
         up_acc[...] += post_stage(half - 1 - j, 2 * j) + post_stage(half + j, 2 * j + 1)
 
     receive(half)
+    send(half + 4)
     nears(0)
-    pump(half + 1)
 
     def step(j, carry):
         receive(half + j)
+
+        @pl.when(half + 4 + j < pairs)
+        def _():
+            send(half + 4 + j)
+
         posts(j - 1)
         nears(j)
 
@@ -294,10 +262,6 @@
         def _():
             for d in range(1, n_samp):
                 gram_copy(d, j // 2 - 1).start()
-
-        @pl.when(j < steps - 1)
-        def _():
-            pump(half + 1 + j)
 
         @pl.when(j == steps // 2)
         def _():
@@ -374,6 +338,19 @@
         return carry
 
     lax.fori_loop(0, steps // 2, finish, 0)
+
+    def sent(c, carry):
+        @pl.when(leaf < n_leaf - 1)
+        def _():
+            to_right(c).wait_send()
+
+        @pl.when(leaf > 0)
+        def _():
+            to_left(c).wait_send()
+
+        return carry
+
+    lax.fori_loop(0, pairs, sent, 0)
     for i in range(3):
         out_copy(i).wait()
     for d in range(1, n_leaf):

time: 42.7 us -> 43.1 us (level)
  Pallas kernels: 41.8 us -> 42.3 us
    pallas_call x1, Pallas kernels: 39.5 us -> 40 us  [shards(): pl.pallas_call(functools.partial(kernel, n_leaf, n_samp, width * n_samp),...]
where the time goes in v6:
time: 43.1 us; the launch traced here: 42.9 us
  Pallas kernels  42.3 us (98%)
  between operations  0.64 us (1%)
    pallas_call x1, Pallas kernels, shards(): pl.pallas_call(functools.partial(kernel, n_leaf, n_samp, width * n_samp),...  40 us
    pallas_call x1, Pallas kernels, shards(): pl.pallas_call(functools.partial(deliver, len(results)), out_shape=tuple(...  2.31 us

profile of v6, /device:TPU:0, one launch (start us, length us, event | category | flops | bytes accessed | tf_op | source)
XLA Modules:
  0.0 42.9 jit_solution(12595289180722327593)
XLA Ops:
  0.6 40.0 %shard_map.103 = (f32[32,64,64]{2,1,0:T(8,128)}, f32[32,1024]{1,0:T(8,128)}, f32[3,64,64]{2,1,0:T(8,128)}) custom-call(s32[8,32]{1,0:T(8,128)} %bitcast.7, s32[32]{0:T(128)} %count_ref.1, bf16[62,4096]{1,0:T(8,128)(2,1)} %inner_hbm.1, bf16[14,4096]{1,0:T(8,128)(2,1)} %upper_hbm.1, bf16[64,4096]{1,0:T(8,128)(2,1)} %bitcast.4, bf16[64,4096]{1,0:T(8,128)(2,1)} %bitcast.5, ...), custom_call_target="tpu_custom_call" | custom-call | tf_op jit(solution)/shard_map/pallas_call | solution.py:392
  40.6 2.3 %shard_map.104 = (f32[32,64,64]{2,1,0:T(8,128)}, f32[32,1024]{1,0:T(8,128)}, f32[1,3,64,64]{3,2,1,0:T(8,128)}) custom-call(f32[32,64,64]{2,1,0:T(8,128)} %get-tuple-element.6.refs_0_, f32[32,1024]{1,0:T(8,128)} %get-tuple-element.7.refs_1_, f32[1,3,64,64]{3,2,1,0:T(8,128)} %bitcast.6), custom_call_target="tpu_custom_call" | custom-call | tf_op jit(solution)/shard_map/pallas_call | solution.py:436

commit v7 on v6

--- a/solution.py
+++ b/solution.py
@@ -35,10 +35,10 @@
 def kernel(
     n_leaf, n_samp, total_columns,
     index_ref, count_ref, inner_hbm, upper_hbm, omega_hbm, samples_hbm, basis_hbm, near_hbm,
-    coeff_hbm, gram_ref, ancestor_ref,
+    coeff_hbm, gram_hbm, ancestor_ref,
     inner_ref, upper_ref, omega_v, samples_v, basis_v, near_v, land_l, land_r, held,
     inner_v, upper_v, paths, ascend, leaf_path, up_acc, up_send, up_recv,
-    gram_send, gram_recv, gram_sum, gram_mix, coeff_v, far_v,
+    gram_send, gram_recv, gram_sum, gram_mix, gram_ref, coeff_v, far_v,
     load_sem, near_sem, send_l, send_r, recv_l, recv_r,
     gram_ssem, gram_rsem, up_ssem, up_rsem, out_sem,
 ):
@@ -104,18 +104,37 @@
         def _():
             to_left(c).start()
 
-    for c in range(half + 1):
+    window = 4
+
+    def pump(c):
+        @pl.when(leaf < n_leaf - 1)
+        def _():
+            to_right(c).wait_send()
+
+        @pl.when(leaf > 0)
+        def _():
+            to_left(c).wait_send()
+
+        @pl.when(c + window < pairs)
+        def _():
+            send(c + window)
+
+    for c in range(window):
         send(c)
 
     load_inner.wait()
     load_upper.wait()
     lines = rank * rank // 128
     for r in range(lines):
+        if r == lines // 2:
+            pump(0)
         for src, dst in ((inner_ref, inner_v), (upper_ref, upper_v)):
             count = src.shape[0]
             tile = src[:, 128 * r:128 * r + 128].astype(F32)
             dst[pl.ds(2 * r, count, stride=rank), :] = tile
             dst[pl.ds(2 * r + 1, count, stride=rank), :] = pltpu.roll(tile, 64, 1)
+
+    pump(1)
 
     eye = (
         lax.broadcasted_iota(jnp.int32, (rank, rank), 0)
@@ -136,6 +155,7 @@
     ascend[...] = jnp.concatenate([rows_high, rows_high, rows_low], axis=1)
     paths[nodes] = eye
 
+    pumped = 2
     for q in reversed(range(leaf_count - 1)):
         mats = inner_v[q * 2 * rank:(q + 1) * 2 * rank, :]
         both = chain_step(paths[leaf_count + q], mats[:, :rank].astype(BF16))
@@ -145,6 +165,11 @@
         else:
             paths[2 * q] = both[:, :rank]
             paths[2 * q + 1] = pltpu.roll(both, 64, 1)[:, :rank]
+        if q % 4 == 0 and pumped <= half:
+            pump(pumped)
+            pumped += 1
+    for c in range(pumped, half + 1):
+        pump(c)
 
     def accept(src, at_held, lo):
         both = src[:, lanes(lo)]
@@ -214,12 +239,8 @@
             to_left(c).wait_recv()
             accept(land_r, 2 * leaf_count, c)
 
-    send(half + 1)
     for c in range(half):
         receive(c)
-        if c == half // 2:
-            send(half + 2)
-    send(half + 3)
 
     span = 4 * part
 
@@ -245,16 +266,11 @@
         up_acc[...] += post_stage(half - 1 - j, 2 * j) + post_stage(half + j, 2 * j + 1)
 
     receive(half)
-    send(half + 4)
     nears(0)
+    pump(half + 1)
 
     def step(j, carry):
         receive(half + j)
-
-        @pl.when(half + 4 + j < pairs)
-        def _():
-            send(half + 4 + j)
-
         posts(j - 1)
         nears(j)
 
@@ -262,6 +278,10 @@
         def _():
             for d in range(1, n_samp):
                 gram_copy(d, j // 2 - 1).start()
+
+        @pl.when(j < steps - 1)
+        def _():
+            pump(half + 1 + j)
 
         @pl.when(j == steps // 2)
         def _():
@@ -278,10 +298,13 @@
     total_high, total_low = split(total + pltpu.roll(total, 64, 1))
     total = dot(ascend[...], jnp.concatenate([total_high, total_low, total_high], axis=0))
     side = rank // 2
+    shares = []
     for h in range(heights):
-        up_send[h * side:(h + 1) * side] = jnp.where(
+        share = jnp.where(
             lower[:side], total[h * rank:h * rank + side], total[h * rank + side:(h + 1) * rank]
         )
+        up_send[h * side:(h + 1) * side] = share.astype(BF16)
+        shares.append(share)
 
     def up_copy(d):
         first = (d.bit_length() - 1) * side
@@ -321,14 +344,16 @@
         gram_mix[pl.ds(lo + 1, pairs, stride=2), :] = odd
         gram_ref[:, 128 * m:128 * m + 128] = gram_mix[lo:lo + leaf_count, :]
 
+    gram_out = pltpu.make_async_copy(gram_ref, gram_hbm, out_sem.at[3])
+    gram_out.start()
     for d in range(1, n_leaf):
         up_copy(d).wait_recv()
     for h in range(heights):
         at = slice(h * side, (h + 1) * side)
-        value = up_send[at, :]
+        value = shares[h]
         for d in range(1, n_leaf):
             if d.bit_length() <= h + 1:
-                value = value + up_recv[d - 1, at, :]
+                value = value + up_recv[d - 1, at, :].astype(F32)
         ancestor_ref[h, 0:side, :] = value[:, :width]
         ancestor_ref[h, side:rank, :] = pltpu.roll(value, 64, 1)[:, :width]
 
@@ -339,18 +364,7 @@
 
     lax.fori_loop(0, steps // 2, finish, 0)
 
-    def sent(c, carry):
-        @pl.when(leaf < n_leaf - 1)
-        def _():
-            to_right(c).wait_send()
-
-        @pl.when(leaf > 0)
-        def _():
-            to_left(c).wait_send()
-
-        return carry
-
-    lax.fori_loop(0, pairs, sent, 0)
+    gram_out.wait()
     for i in range(3):
         out_copy(i).wait()
     for d in range(1, n_leaf):
@@ -397,7 +411,7 @@
             jax.ShapeDtypeStruct((heights, rank, width), F32),
         ),
         in_specs=[smem, smem, hbm, hbm, hbm, hbm, hbm, hbm],
-        out_specs=(hbm, vmem, vmem),
+        out_specs=(hbm, hbm, vmem),
         scratch_shapes=[
             pltpu.VMEM(inner_transfer.shape, BF16),
             pltpu.VMEM(upper_transfer.shape, BF16),
@@ -414,19 +428,20 @@
             pltpu.VMEM((heights * rank, 3 * rank), BF16),
             pltpu.VMEM((pairs, rank, 384), BF16),
             pltpu.VMEM((rank, 128), F32),
-            pltpu.VMEM((heights * rank // 2, 128), F32),
-            pltpu.VMEM((n_leaf - 1, heights * rank // 2, 128), F32),
+            pltpu.VMEM((heights * rank // 2, 128), BF16),
+            pltpu.VMEM((n_leaf - 1, heights * rank // 2, 128), BF16),
             pltpu.VMEM((n_samp, pairs * part, 128), wire),
             pltpu.VMEM((n_samp - 1, pairs * part, 128), wire),
             pltpu.VMEM((pairs * part, 128), F32),
             pltpu.VMEM((part // 2 * leaf_count, 128), F32),
+            pltpu.VMEM((leaf_count, part * rank), F32),
             pltpu.VMEM((leaf_count, rank, width), F32),
             pltpu.VMEM((pairs, leaf_size, leaf_size), BF16),
             dma((5,)), dma,
             dma((pairs,)), dma((pairs,)), dma((pairs,)), dma((pairs,)),
             dma((n_samp - 1, steps // 2)), dma((n_samp - 1, steps // 2)),
             dma((n_leaf - 1,)), dma((n_leaf - 1,)),
-            dma((3,)),
+            dma((4,)),
         ],
         compiler_params=pltpu.CompilerParams(
             collective_id=0, has_side_effects=True, vmem_limit_bytes=56 * 1024 * 1024

time: 43.1 us -> 41.3 us (0.958)
  Pallas kernels: 42.3 us -> 40.5 us
    pallas_call x1, Pallas kernels: 40 us -> 38.1 us  [shards(): pl.pallas_call(functools.partial(kernel, n_leaf, n_samp, width * n_samp),...]
where the time goes in v7:
time: 41.3 us; the launch traced here: 41.1 us
  Pallas kernels  40.5 us (98%)
  between operations  0.64 us (2%)
    pallas_call x1, Pallas kernels, shards(): pl.pallas_call(functools.partial(kernel, n_leaf, n_samp, width * n_samp),...  38.1 us
    pallas_call x1, Pallas kernels, shards(): pl.pallas_call(functools.partial(deliver, len(results)), out_shape=tuple(...  2.31 us

profile of v7, /device:TPU:0, one launch (start us, length us, event | category | flops | bytes accessed | tf_op | source)
XLA Modules:
  0.0 41.1 jit_solution(1252115682908552906)
XLA Ops:
  0.6 38.1 %shard_map.103 = (f32[32,64,64]{2,1,0:T(8,128)}, f32[32,1024]{1,0:T(8,128)}, f32[3,64,64]{2,1,0:T(8,128)}) custom-call(s32[8,32]{1,0:T(8,128)} %bitcast.7, s32[32]{0:T(128)} %count_ref.1, bf16[62,4096]{1,0:T(8,128)(2,1)} %inner_hbm.1, bf16[14,4096]{1,0:T(8,128)(2,1)} %upper_hbm.1, bf16[64,4096]{1,0:T(8,128)(2,1)} %bitcast.4, bf16[64,4096]{1,0:T(8,128)(2,1)} %bitcast.5, ...), custom_call_target="tpu_custom_call" | custom-call | tf_op jit(solution)/shard_map/pallas_call | solution.py:406
  38.8 2.3 %shard_map.104 = (f32[32,64,64]{2,1,0:T(8,128)}, f32[32,1024]{1,0:T(8,128)}, f32[1,3,64,64]{3,2,1,0:T(8,128)}) custom-call(f32[32,64,64]{2,1,0:T(8,128)} %get-tuple-element.6.refs_0_, f32[32,1024]{1,0:T(8,128)} %get-tuple-element.7.refs_1_, f32[1,3,64,64]{3,2,1,0:T(8,128)} %bitcast.6), custom_call_target="tpu_custom_call" | custom-call | tf_op jit(solution)/shard_map/pallas_call | solution.py:451

commit v8 on v7

--- a/solution.py
+++ b/solution.py
@@ -279,9 +279,7 @@
             for d in range(1, n_samp):
                 gram_copy(d, j // 2 - 1).start()
 
-        @pl.when(j < steps - 1)
-        def _():
-            pump(half + 1 + j)
+        pump(half + 1 + j)
 
         @pl.when(j == steps // 2)
         def _():
@@ -289,10 +287,11 @@
 
         return carry
 
-    lax.fori_loop(1, steps, step, 0)
+    lax.fori_loop(1, steps - 1, step, 0)
+    posts(steps - 2)
+    receive(pairs - 1)
+    nears(steps - 1)
     posts(steps - 1)
-    for d in range(1, n_samp):
-        gram_copy(d, steps // 2 - 1).start()
 
     total = up_acc[...]
     total_high, total_low = split(total + pltpu.roll(total, 64, 1))
@@ -315,8 +314,10 @@
             device_id=(leaf ^ d, samp), device_id_type=MESH,
         )
 
-    for d in range(1, n_leaf):
+    for d in reversed(range(1, n_leaf)):
         up_copy(d).start()
+    for d in range(1, n_samp):
+        gram_copy(d, steps // 2 - 1).start()
     out_copy(1).start()
     out_copy(2).start()
 

time: 41.3 us -> 40.8 us (0.988)
  Pallas kernels: 40.5 us -> 39.9 us
    pallas_call x1, Pallas kernels: 38.1 us -> 37.6 us  [shards(): pl.pallas_call(functools.partial(kernel, n_leaf, n_samp, width * n_samp),...]
where the time goes in v8:
time: 40.8 us; the launch traced here: 40.6 us
  Pallas kernels  39.9 us (98%)
  between operations  0.64 us (2%)
    pallas_call x1, Pallas kernels, shards(): pl.pallas_call(functools.partial(kernel, n_leaf, n_samp, width * n_samp),...  37.6 us
    pallas_call x1, Pallas kernels, shards(): pl.pallas_call(functools.partial(deliver, len(results)), out_shape=tuple(...  2.31 us

profile of v8, /device:TPU:0, one launch (start us, length us, event | category | flops | bytes accessed | tf_op | source)
XLA Modules:
  0.0 40.6 jit_solution(17064216644056713109)
XLA Ops:
  0.6 37.6 %shard_map.103 = (f32[32,64,64]{2,1,0:T(8,128)}, f32[32,1024]{1,0:T(8,128)}, f32[3,64,64]{2,1,0:T(8,128)}) custom-call(s32[8,32]{1,0:T(8,128)} %bitcast.7, s32[32]{0:T(128)} %count_ref.1, bf16[62,4096]{1,0:T(8,128)(2,1)} %inner_hbm.1, bf16[14,4096]{1,0:T(8,128)(2,1)} %upper_hbm.1, bf16[64,4096]{1,0:T(8,128)(2,1)} %bitcast.4, bf16[64,4096]{1,0:T(8,128)(2,1)} %bitcast.5, ...), custom_call_target="tpu_custom_call" | custom-call | tf_op jit(solution)/shard_map/pallas_call | solution.py:407
  38.2 2.3 %shard_map.104 = (f32[32,64,64]{2,1,0:T(8,128)}, f32[32,1024]{1,0:T(8,128)}, f32[1,3,64,64]{3,2,1,0:T(8,128)}) custom-call(f32[32,64,64]{2,1,0:T(8,128)} %get-tuple-element.6.refs_0_, f32[32,1024]{1,0:T(8,128)} %get-tuple-element.7.refs_1_, f32[1,3,64,64]{3,2,1,0:T(8,128)} %bitcast.6), custom_call_target="tpu_custom_call" | custom-call | tf_op jit(solution)/shard_map/pallas_call | solution.py:452
